TPU v7x, 32 devices: a whole 2x2x4 slice. The times are simulated.
32 devices in a mesh: replica: 16 (over z, x, core), group: 2 (over y).
Axes of the slice: x: 2, y: 2, z: 4, core: 2. Of those that a mesh axis runs over, the one named last changes fastest.
Arguments:
- tokens: bfloat16 [16384, 1024], P(('replica', 'group')), may hold values from -6 to 6
- cotangent: bfloat16 [16384, 1024], P(('replica', 'group')), may hold values from -6 to 6
- routes: int32 [16384, 8], P(('replica', 'group')), may hold values from 0 to 15, all different within a row; in each aligned block of 512 rows (0 to 511, 512 to 1023, ...) at most 320 rows name the same one
- first_gain: bfloat16 [1024], P('group'), may hold values from 0.5 to 1.5
- query_weight: bfloat16 [1024, 1024], P('group'), may hold values from -0.625 to 0.625
- key_weight: bfloat16 [1024, 512], P('group'), may hold values from -0.625 to 0.625
- value_weight: bfloat16 [1024, 512], P('group'), may hold values from -0.75 to 0.75
- output_weight: bfloat16 [1024, 1024], P('group'), may hold values from -0.75 to 0.75
- second_gain: bfloat16 [1024], P('group'), may hold values from 0.5 to 1.5
- router_weight: bfloat16 [1024, 16], P('group'), may hold values from -0.09375 to 0.09375
- gate_weight: bfloat16 [16, 1024, 512], P('group'), may hold values from -0.1875 to 0.1875
- up_weight: bfloat16 [16, 1024, 512], P('group'), may hold values from -0.1875 to 0.1875
- down_weight: bfloat16 [16, 512, 1024], P('group'), may hold values from -2 to 2
Outputs:
- layer_output: bfloat16 [16384, 1024], P(('replica', 'group'))
- tokens_grad: float32 [16384, 1024], P(('replica', 'group'))
- first_gain_grad: float32 [1024], P('group')
- query_grad: float32 [1024, 1024], P('group')
- key_grad: float32 [1024, 512], P('group')
- value_grad: float32 [1024, 512], P('group')
- output_grad: float32 [1024, 1024], P('group')
- second_gain_grad: float32 [1024], P('group')
- router_grad: float32 [1024, 16], P('group')
- gate_grad: float32 [16, 1024, 512], P('group')
- up_grad: float32 [16, 1024, 512], P('group')
- down_grad: float32 [16, 512, 1024], P('group')
Inputs may be any that keep to these rules, and one draw needn't show every extreme that they name: `routes`: each row names 8 different experts. Within the tokens of one device no expert is named by more than 320 tokens, and in some device one expert is named by exactly 320.
All inputs are finite; a program needn't handle non-finite values.
Results may differ from a plain program's by a relative error of at most 0.02.
Values may be sent and summed in bfloat16 or wider, within the bound.
A program may use at most 320 MiB of HBM per device.

v0:
```python
import jax
import jax.numpy as jnp
from jax import lax
from jax.sharding import PartitionSpec as P

HQ = 16
KV = 8
HD = 64
FF = 512
E = 16
TOPK = 8
GRP = 2
CAP = 320


norm_eps = 1e-06
residual_scale = 0.22
score_scale = 0.015625
rope_base = 10000.0
masked_value = -1e30


def rope_tables(length):
    positions = jnp.arange(length, dtype=jnp.float32)
    inverse = rope_base ** (-jnp.arange(0, HD, 2, dtype=jnp.float32) / HD)
    angles = positions[:, None] * inverse[None, :]
    cosine_table = jnp.cos(angles)
    sine_table = jnp.sin(angles)
    return (
        jnp.concatenate([cosine_table, cosine_table], -1),
        jnp.concatenate([sine_table, sine_table], -1),
    )


def rotate(values, cosine_table, sine_table):
    half_width = values.shape[-1] // 2
    turned = jnp.concatenate([-values[..., half_width:], values[..., :half_width]], -1)
    return values * cosine_table[:, None, :] + turned * sine_table[:, None, :]


def rotate_back(grads, cosine_table, sine_table):
    half_width = grads.shape[-1] // 2
    with_sine = grads * sine_table[:, None, :]
    turned = jnp.concatenate([with_sine[..., half_width:], -with_sine[..., :half_width]], -1)
    return grads * cosine_table[:, None, :] + turned


def slot_table(routes_dev):
    flat_routes = routes_dev.reshape(-1)
    one_hot = (flat_routes[:, None] == jnp.arange(E, dtype=jnp.int32)[None, :]).astype(jnp.int32)
    earlier = jnp.cumsum(one_hot, axis=0) - one_hot
    position = jnp.sum(earlier * one_hot, axis=1)
    slot_of = flat_routes * CAP + position
    entries = flat_routes.shape[0]
    source = (
        jnp.full((E * CAP,), entries, jnp.int32)
        .at[slot_of]
        .set(jnp.arange(entries, dtype=jnp.int32))
    )
    return (slot_of, source)


def expert_forward(inputs, gate_part, up_part, down_part, leading):
    gate_pre = jnp.einsum(
        leading + "ecd,edf->" + leading + "ecf",
        inputs,
        gate_part,
        preferred_element_type=jnp.float32,
    )
    up_pre = jnp.einsum(
        leading + "ecd,edf->" + leading + "ecf", inputs, up_part, preferred_element_type=jnp.float32
    )
    hidden = (jax.nn.silu(gate_pre) * up_pre).astype(jnp.bfloat16)
    produced = jnp.einsum(
        leading + "ecf,efd->" + leading + "ecd",
        hidden,
        down_part,
        preferred_element_type=jnp.float32,
    )
    return produced.astype(jnp.bfloat16)


def expert_backward(inputs, grads_out, gate_part, up_part, down_part, leading):
    gate_pre = jnp.einsum(
        leading + "ecd,edf->" + leading + "ecf",
        inputs,
        gate_part,
        preferred_element_type=jnp.float32,
    )
    up_pre = jnp.einsum(
        leading + "ecd,edf->" + leading + "ecf", inputs, up_part, preferred_element_type=jnp.float32
    )
    sigmoid_gate = jax.nn.sigmoid(gate_pre)
    swish_gate = gate_pre * sigmoid_gate
    hidden = (swish_gate * up_pre).astype(jnp.bfloat16)
    grad_hidden = jnp.einsum(
        leading + "ecd,efd->" + leading + "ecf",
        grads_out,
        down_part,
        preferred_element_type=jnp.float32,
    )
    grad_gate = (
        grad_hidden * up_pre * sigmoid_gate * (1.0 + gate_pre * (1.0 - sigmoid_gate))
    ).astype(jnp.bfloat16)
    grad_up = (grad_hidden * swish_gate).astype(jnp.bfloat16)
    down_part_grad = jnp.einsum(
        leading + "ecf," + leading + "ecd->efd",
        hidden,
        grads_out,
        preferred_element_type=jnp.float32,
    )
    gate_part_grad = jnp.einsum(
        leading + "ecd," + leading + "ecf->edf",
        inputs,
        grad_gate,
        preferred_element_type=jnp.float32,
    )
    up_part_grad = jnp.einsum(
        leading + "ecd," + leading + "ecf->edf", inputs, grad_up, preferred_element_type=jnp.float32
    )
    grad_inputs = jnp.einsum(
        leading + "ecf,edf->" + leading + "ecd",
        grad_gate,
        gate_part,
        preferred_element_type=jnp.float32,
    )
    grad_inputs = grad_inputs + jnp.einsum(
        leading + "ecf,edf->" + leading + "ecd",
        grad_up,
        up_part,
        preferred_element_type=jnp.float32,
    )
    return (grad_inputs, gate_part_grad, up_part_grad, down_part_grad)


def head_slices(queries, key_rows, values, group_index, length):
    query_block = lax.dynamic_slice_in_dim(queries, group_index * GRP * HD, GRP * HD, 1).reshape(
        length, GRP, HD
    )
    key_block = lax.dynamic_slice_in_dim(key_rows, group_index * HD, HD, 1)
    value_block = lax.dynamic_slice_in_dim(values, group_index * HD, HD, 1)
    return (query_block, key_block, value_block)


def attend_forward(queries, key_rows, values, causal):
    length = queries.shape[0]

    def one_group(group_index):
        query_block, key_block, value_block = head_slices(
            queries, key_rows, values, group_index, length
        )
        scores = (
            jnp.einsum("sgd,td->gst", query_block, key_block, preferred_element_type=jnp.float32)
            * score_scale
        )
        scores = jnp.where(causal[None], scores, masked_value)
        row_peak = jnp.max(scores, axis=-1, keepdims=True)
        exponent = jnp.exp(scores - row_peak)
        row_total = jnp.sum(exponent, axis=-1, keepdims=True)
        probability = (exponent / row_total).astype(jnp.bfloat16)
        block_mix = jnp.einsum(
            "gst,td->sgd", probability, value_block, preferred_element_type=jnp.float32
        )
        return (block_mix.reshape(length, GRP * HD), (row_peak + jnp.log(row_total))[..., 0])

    blocks, log_sums = lax.map(one_group, jnp.arange(KV, dtype=jnp.int32))
    return (blocks.transpose(1, 0, 2).reshape(length, HQ * HD), log_sums)


def attend_backward(queries, key_rows, values, grad_mix, log_sums, causal):
    length = queries.shape[0]

    def one_group(paired):
        group_index, group_sums = paired
        query_block, key_block, value_block = head_slices(
            queries, key_rows, values, group_index, length
        )
        grad_block = lax.dynamic_slice_in_dim(
            grad_mix, group_index * GRP * HD, GRP * HD, 1
        ).reshape(length, GRP, HD)
        scores = (
            jnp.einsum("sgd,td->gst", query_block, key_block, preferred_element_type=jnp.float32)
            * score_scale
        )
        scores = jnp.where(causal[None], scores, masked_value)
        probability = jnp.exp(scores - group_sums[..., None])
        rounded = probability.astype(jnp.bfloat16)
        grad_prob = jnp.einsum(
            "sgd,td->gst", grad_block, value_block, preferred_element_type=jnp.float32
        )
        grad_scores = probability * (
            grad_prob - jnp.sum(probability * grad_prob, axis=-1, keepdims=True)
        )
        grad_scores = grad_scores.astype(jnp.bfloat16)
        grad_query = (
            jnp.einsum("gst,td->sgd", grad_scores, key_block, preferred_element_type=jnp.float32)
            * score_scale
        )
        grad_key = (
            jnp.einsum("gst,sgd->td", grad_scores, query_block, preferred_element_type=jnp.float32)
            * score_scale
        )
        grad_value = jnp.einsum(
            "gst,sgd->td", rounded, grad_block, preferred_element_type=jnp.float32
        )
        return (grad_query.reshape(length, GRP * HD), grad_key, grad_value)

    query_parts, key_parts, value_parts = lax.map(
        one_group, (jnp.arange(KV, dtype=jnp.int32), log_sums)
    )
    return (
        query_parts.transpose(1, 0, 2).reshape(length, HQ * HD),
        key_parts.transpose(1, 0, 2).reshape(length, KV * HD),
        value_parts.transpose(1, 0, 2).reshape(length, KV * HD),
    )


def shards(
    tokens,
    cotangent,
    routes,
    first_gain,
    query_weight,
    key_weight,
    value_weight,
    output_weight,
    second_gain,
    router_weight,
    gate_weight,
    up_weight,
    down_weight,
):
    length = tokens.shape[0]
    width = tokens.shape[1]
    gain_one, query_full, key_full, value_full, output_full, gain_two, router_full = (
        lax.all_gather(first_gain, "group", axis=0, tiled=True),
        lax.all_gather(query_weight, "group", axis=0, tiled=True),
        lax.all_gather(key_weight, "group", axis=0, tiled=True),
        lax.all_gather(value_weight, "group", axis=0, tiled=True),
        lax.all_gather(output_weight, "group", axis=0, tiled=True),
        lax.all_gather(second_gain, "group", axis=0, tiled=True),
        lax.all_gather(router_weight, "group", axis=0, tiled=True),
    )
    tokens_float = tokens.astype(jnp.float32)
    scale_one = lax.rsqrt(jnp.mean(tokens_float * tokens_float, axis=-1, keepdims=True) + norm_eps)
    normed_one = (tokens_float * scale_one * gain_one.astype(jnp.float32)).astype(jnp.bfloat16)
    cosine_table, sine_table = rope_tables(length)
    query_pre = jnp.dot(normed_one, query_full, preferred_element_type=jnp.float32).reshape(
        length, HQ, HD
    )
    queries = (
        rotate(query_pre, cosine_table, sine_table).astype(jnp.bfloat16).reshape(length, HQ * HD)
    )
    key_pre = jnp.dot(normed_one, key_full, preferred_element_type=jnp.float32).reshape(
        length, KV, HD
    )
    key_rows = (
        rotate(key_pre, cosine_table, sine_table).astype(jnp.bfloat16).reshape(length, KV * HD)
    )
    values = jnp.dot(normed_one, value_full, preferred_element_type=jnp.float32).astype(
        jnp.bfloat16
    )
    causal = jnp.arange(length)[:, None] >= jnp.arange(length)[None, :]
    attention_raw, log_sums = attend_forward(queries, key_rows, values, causal)
    attention_mix = attention_raw.astype(jnp.bfloat16)
    attention_out = jnp.dot(attention_mix, output_full, preferred_element_type=jnp.float32)
    resid = tokens_float + residual_scale * attention_out
    scale_two = lax.rsqrt(jnp.mean(resid * resid, axis=-1, keepdims=True) + norm_eps)
    normed_two = (resid * scale_two * gain_two.astype(jnp.float32)).astype(jnp.bfloat16)
    logits = jnp.dot(normed_two, router_full, preferred_element_type=jnp.float32)
    route_gates = jax.nn.softmax(jnp.take_along_axis(logits, routes, axis=1), axis=-1)
    slot_of, source = slot_table(routes)
    padded = jnp.concatenate([normed_two, jnp.zeros((1, width), jnp.bfloat16)], 0)
    expert_in = padded[source // TOPK].reshape(E, CAP, width)
    gate_part = lax.all_gather(gate_weight, "group", axis=0, tiled=True)
    up_part = lax.all_gather(up_weight, "group", axis=0, tiled=True)
    down_part = lax.all_gather(down_weight, "group", axis=0, tiled=True)
    inputs = expert_in
    produced = expert_forward(inputs, gate_part, up_part, down_part, "")
    expert_out = lax.dynamic_update_slice_in_dim(
        jnp.zeros((E, CAP, width), jnp.bfloat16), produced, jnp.int32(0), 0
    )
    picked = expert_out.reshape(E * CAP, width)[slot_of].reshape(length, TOPK, width)
    moe_out = jnp.sum(route_gates[:, :, None] * picked, axis=1)
    layer_output = (resid + residual_scale * moe_out).astype(jnp.bfloat16)
    gain_back, query_back, key_back, value_back, output_back, gain_two_back, router_back = (
        lax.all_gather(first_gain, "group", axis=0, tiled=True),
        lax.all_gather(query_weight, "group", axis=0, tiled=True),
        lax.all_gather(key_weight, "group", axis=0, tiled=True),
        lax.all_gather(value_weight, "group", axis=0, tiled=True),
        lax.all_gather(output_weight, "group", axis=0, tiled=True),
        lax.all_gather(second_gain, "group", axis=0, tiled=True),
        lax.all_gather(router_weight, "group", axis=0, tiled=True),
    )
    grad_out = cotangent.astype(jnp.float32)
    grad_moe = residual_scale * grad_out
    grad_gates = jnp.sum(picked * grad_moe[:, None, :], axis=-1)
    grad_rows = (
        (route_gates[:, :, None] * grad_moe[:, None, :])
        .astype(jnp.bfloat16)
        .reshape(length * TOPK, width)
    )
    grad_slots = jnp.concatenate([grad_rows, jnp.zeros((1, width), jnp.bfloat16)], 0)[
        source
    ].reshape(E, CAP, width)
    first = jnp.int32(0)
    grad_in = jnp.zeros((E, CAP, width), jnp.float32)
    gate_acc = jnp.zeros((E, width, FF), jnp.float32)
    up_acc = jnp.zeros((E, width, FF), jnp.float32)
    down_acc = jnp.zeros((E, FF, width), jnp.float32)
    gate_part = lax.all_gather(gate_weight, "group", axis=0, tiled=True)
    up_part = lax.all_gather(up_weight, "group", axis=0, tiled=True)
    down_part = lax.all_gather(down_weight, "group", axis=0, tiled=True)
    inputs = expert_in
    grad_inputs, gate_part_grad, up_part_grad, down_part_grad = expert_backward(
        inputs, grad_slots, gate_part, up_part, down_part, ""
    )
    grad_expert_in = lax.dynamic_update_slice_in_dim(grad_in, grad_inputs, first, 0)
    gate_whole = lax.dynamic_update_slice_in_dim(gate_acc, gate_part_grad, first, 0)
    up_whole = lax.dynamic_update_slice_in_dim(up_acc, up_part_grad, first, 0)
    down_whole = lax.dynamic_update_slice_in_dim(down_acc, down_part_grad, first, 0)
    gate_grad, up_grad, down_grad = (
        lax.psum_scatter(
            gate_whole.astype(jnp.bfloat16), "group", scatter_dimension=0, tiled=True
        ).astype(jnp.float32),
        lax.psum_scatter(
            up_whole.astype(jnp.bfloat16), "group", scatter_dimension=0, tiled=True
        ).astype(jnp.float32),
        lax.psum_scatter(
            down_whole.astype(jnp.bfloat16), "group", scatter_dimension=0, tiled=True
        ).astype(jnp.float32),
    )
    grad_from_experts = jnp.sum(
        grad_expert_in.reshape(E * CAP, width)[slot_of].reshape(length, TOPK, width), axis=1
    )
    grad_chosen = route_gates * (
        grad_gates - jnp.sum(route_gates * grad_gates, axis=-1, keepdims=True)
    )
    routing_hot = (routes[:, :, None] == jnp.arange(E, dtype=jnp.int32)[None, None, :]).astype(
        jnp.float32
    )
    grad_logits = jnp.sum(routing_hot * grad_chosen[:, :, None], axis=1).astype(jnp.bfloat16)
    router_grad = jnp.einsum(
        "sd,se->de", normed_two, grad_logits, preferred_element_type=jnp.float32
    )
    grad_normed_two = grad_from_experts + jnp.einsum(
        "se,de->sd", grad_logits, router_back, preferred_element_type=jnp.float32
    )
    second_gain_grad = jnp.sum(grad_normed_two * resid * scale_two, axis=0)
    weighted_two = grad_normed_two * gain_two_back.astype(jnp.float32)
    grad_resid = (
        grad_out
        + scale_two * weighted_two
        - resid * scale_two**3 * jnp.mean(weighted_two * resid, axis=-1, keepdims=True)
    )
    grad_attention = (residual_scale * grad_resid).astype(jnp.bfloat16)
    output_grad = jnp.einsum(
        "sk,sd->kd", attention_mix, grad_attention, preferred_element_type=jnp.float32
    )
    grad_mix = jnp.einsum(
        "sd,kd->sk", grad_attention, output_back, preferred_element_type=jnp.float32
    ).astype(jnp.bfloat16)
    grad_query_rot, grad_key_rot, grad_value_raw = attend_backward(
        queries, key_rows, values, grad_mix, log_sums, causal
    )
    grad_query_pre = rotate_back(grad_query_rot.reshape(length, HQ, HD), cosine_table, sine_table)
    grad_query_pre = grad_query_pre.reshape(length, HQ * HD).astype(jnp.bfloat16)
    grad_key_pre = rotate_back(grad_key_rot.reshape(length, KV, HD), cosine_table, sine_table)
    grad_key_pre = grad_key_pre.reshape(length, KV * HD).astype(jnp.bfloat16)
    grad_value_pre = grad_value_raw.astype(jnp.bfloat16)
    query_grad = jnp.einsum(
        "sd,sk->dk", normed_one, grad_query_pre, preferred_element_type=jnp.float32
    )
    key_grad = jnp.einsum("sd,sk->dk", normed_one, grad_key_pre, preferred_element_type=jnp.float32)
    value_grad = jnp.einsum(
        "sd,sk->dk", normed_one, grad_value_pre, preferred_element_type=jnp.float32
    )
    grad_normed_one = jnp.einsum(
        "sk,dk->sd", grad_query_pre, query_back, preferred_element_type=jnp.float32
    )
    grad_normed_one = grad_normed_one + jnp.einsum(
        "sk,dk->sd", grad_key_pre, key_back, preferred_element_type=jnp.float32
    )
    grad_normed_one = grad_normed_one + jnp.einsum(
        "sk,dk->sd", grad_value_pre, value_back, preferred_element_type=jnp.float32
    )
    first_gain_grad = jnp.sum(grad_normed_one * tokens_float * scale_one, axis=0)
    weighted_one = grad_normed_one * gain_back.astype(jnp.float32)
    tokens_grad = (
        grad_resid
        + scale_one * weighted_one
        - tokens_float
        * scale_one**3
        * jnp.mean(weighted_one * tokens_float, axis=-1, keepdims=True)
    )
    gain_one_own, query_own, key_own, value_own, output_own, gain_two_own, router_own = (
        lax.psum_scatter(
            first_gain_grad.astype(jnp.bfloat16), "group", scatter_dimension=0, tiled=True
        ).astype(jnp.float32),
        lax.psum_scatter(
            query_grad.astype(jnp.bfloat16), "group", scatter_dimension=0, tiled=True
        ).astype(jnp.float32),
        lax.psum_scatter(
            key_grad.astype(jnp.bfloat16), "group", scatter_dimension=0, tiled=True
        ).astype(jnp.float32),
        lax.psum_scatter(
            value_grad.astype(jnp.bfloat16), "group", scatter_dimension=0, tiled=True
        ).astype(jnp.float32),
        lax.psum_scatter(
            output_grad.astype(jnp.bfloat16), "group", scatter_dimension=0, tiled=True
        ).astype(jnp.float32),
        lax.psum_scatter(
            second_gain_grad.astype(jnp.bfloat16), "group", scatter_dimension=0, tiled=True
        ).astype(jnp.float32),
        lax.psum_scatter(
            router_grad.astype(jnp.bfloat16), "group", scatter_dimension=0, tiled=True
        ).astype(jnp.float32),
    )
    summed = (
        lax.psum(gain_one_own.astype(jnp.bfloat16), "replica").astype(jnp.float32),
        lax.psum(query_own.astype(jnp.bfloat16), "replica").astype(jnp.float32),
        lax.psum(key_own.astype(jnp.bfloat16), "replica").astype(jnp.float32),
        lax.psum(value_own.astype(jnp.bfloat16), "replica").astype(jnp.float32),
        lax.psum(output_own.astype(jnp.bfloat16), "replica").astype(jnp.float32),
        lax.psum(gain_two_own.astype(jnp.bfloat16), "replica").astype(jnp.float32),
        lax.psum(router_own.astype(jnp.bfloat16), "replica").astype(jnp.float32),
        lax.psum(gate_grad.astype(jnp.bfloat16), "replica").astype(jnp.float32),
        lax.psum(up_grad.astype(jnp.bfloat16), "replica").astype(jnp.float32),
        lax.psum(down_grad.astype(jnp.bfloat16), "replica").astype(jnp.float32),
    )
    return (
        layer_output,
        tokens_grad,
        summed[0],
        summed[1],
        summed[2],
        summed[3],
        summed[4],
        summed[5],
        summed[6],
        summed[7],
        summed[8],
        summed[9],
    )


def solution(mesh):
    return jax.shard_map(
        shards,
        mesh=mesh,
        in_specs=(
            P(("replica", "group"), None),
            P(("replica", "group"), None),
            P(("replica", "group"), None),
            P("group"),
            P("group", None),
            P("group", None),
            P("group", None),
            P("group", None),
            P("group"),
            P("group", None),
            P("group", None, None),
            P("group", None, None),
            P("group", None, None),
        ),
        out_specs=(
            P(("replica", "group"), None),
            P(("replica", "group"), None),
            P("group"),
            P("group", None),
            P("group", None),
            P("group", None),
            P("group", None),
            P("group"),
            P("group", None),
            P("group", None, None),
            P("group", None, None),
            P("group", None, None),
        ),
        check_vma=False,
    )
```

profile of v0, /device:TPU:0, one launch (start us, length us, event | category | flops | bytes accessed | tf_op | source)
XLA Modules:
  0.0 2228.2 jit_solution(8827446554895176833)
XLA Ops:
  14.4 5.3 all-gather
  22.2 4.3 all-gather.1
  26.5 4.7 all_gather.46
  33.1 4.6 reduce-window.6
  39.7 15.5 scatter_custom_fusion
  58.2 3.1 convolution_convert_fusion.9
  63.4 28.2 %all-gather.14.cloned.1.call-done = bf16[1024,1024]{1,0:T(8,128)(2,1)} async-done(((bf16[512,1024]{1,0:T(8,128)(2,1)}), bf16[1024,1024]{1,0:T(8,128)(2,1)}) %all-gather.14.cloned.1.call-update) | async-done | bytes 2097168 | tf_op jit(solution)/shard_map/all_gather | solution.py:237
  91.6 4.5 fusion.71
  96.2 3.0 copy.128
  105.7 4.4 add_convert_fusion.1
  112.3 51.5 %while.34 = (s32[]{:T(128)}, bf16[8,512,128]{1,2,0:T(8,128)(2,1)}, f32[8,2,512]{2,1,0:T(2,128)}, s32[8]{0:T(128)S(1)}, bf16[512,512]{0,1:T(8,128)(2,1)}, /*index...) while((s32[]{:T(128)}, bf16[8,512,128]{1,2,0:T(8,128)(2,1)}, ...), condition=%wide.region_4.5_spmd.clone.clone, body=%wide.region_1.4_spmd.clone.sunk.clone | while | flops 138673152 | bytes 7767249 | solution.py:166
  163.8 3.8 multiply_reduce_fusion.2
  170.5 33.0 %gather_fusion.4 = f32[4096]{0:T(1024)S(1)} fusion(f32[512,16]{0,1:T(8,128)S(1)} %fusion.79, s32[4096]{0:T(1024)S(1)} %reshape.338), kind=kCustom, calls=%fused_computation.4 | custom fusion | bytes 65536 | tf_op jit(solution)/shard_map/jit(take_along_axis)/gather | solution.py:271
  205.5 4.0 fusion.34
  209.4 7.8 concatenate.31
  217.2 30.3 %gather_fusion.2 = bf16[5120,1024]{1,0:T(8,128)(2,1)} fusion(bf16[4097,1024]{1,0:T(8,128)(2,1)} %concatenate.31, s32[5120]{0:T(1024)S(1)} %get-tuple-element.467), kind=kCustom, calls=%fused_computation.2 | custom fusion | bytes 20992000 | tf_op jit(solution)/shard_map/gather | solution.py:303
  247.5 22.5 %gather_fusion = bf16[5120,1024]{1,0:T(8,128)(2,1)} fusion(bf16[513,1024]{1,0:T(8,128)(2,1)S(1)} %concatenate.30, s32[5120]{0:T(1024)S(1)} %get-tuple-element.468), kind=kCustom, calls=%fused_computation | custom fusion | bytes 20992000 | tf_op jit(solution)/shard_map/gather | solution.py:274
  270.0 56.5 %all-gather.18.cloned.1.call-done = bf16[16,1024,512]{2,1,0:T(8,128)(2,1)} async-done(((bf16[8,1024,512]{2,1,0:T(8,128)(2,1)}), bf16[16,1024,512]{2,1,0:T(8,128)(2,1)}) %all-gather.18.cloned.1.call-update) | async-done | bytes 16777232 | tf_op jit(solution)/shard_map/all_gather | solution.py:275
  326.5 16.5 fusion.80
  343.0 183.8 %all-gather.20.cloned.1.call-done = bf16[16,1024,512]{2,1,0:T(8,128)(2,1)} async-done(((bf16[8,1024,512]{2,1,0:T(8,128)(2,1)}), bf16[16,1024,512]{2,1,0:T(8,128)(2,1)}) %all-gather.20.cloned.1.call-update) | async-done | bytes 16777232 | tf_op jit(solution)/shard_map/all_gather | solution.py:276
  526.8 16.7 fusion.81
  543.5 183.7 %all-gather.22.cloned.1.call-done = bf16[16,512,1024]{2,1,0:T(8,128)(2,1)} async-done(((bf16[8,512,1024]{2,1,0:T(8,128)(2,1)}), bf16[16,512,1024]{2,1,0:T(8,128)(2,1)}) %all-gather.22.cloned.1.call-update) | async-done | bytes 16777232 | tf_op jit(solution)/shard_map/all_gather | solution.py:277
  727.2 26.1 %multiply_convert_fusion = (bf16[16,320,512]{2,1,0:T(8,128)(2,1)}, bf16[16,320,512]{2,1,0:T(8,128)(2,1)}, bf16[16,320,512]{2,1,0:T(8,128)(2,1)}) fusion(f32[16,320,512]{2,1,0:T(8,128)} %fusion.80, f32[16,320,512]{2,1,0:T(8,128)} %fusion.81, bf16[16,320,1024]{2,1,0:T(8,128)(2,1)} %bitcast.283, bf16[16,512,1024]{2,1,0:T(8,128)(2,1)} %all-gather.22.cloned.1.call-done), kind=kOutput, calls=%fused_computation.61 | convolution fusion | flops 5408030720 | bytes 63963136 | tf_op jit(solution)/shard_map/ecd,efd->ecf/dot_general | solution.py:96
  753.3 14.8 convolution_convert_fusion.3
  768.1 26.1 %gather_fusion.1 = bf16[4096,1024]{1,0:T(8,128)(2,1)} fusion(bf16[5120,1024]{1,0:T(8,128)(2,1)} %bitcast.278, s32[4096]{0:T(1024)S(1)} %copy-done.32), kind=kCustom, calls=%fused_computation.1 | custom fusion | bytes 16793600 | tf_op jit(solution)/shard_map/gather | solution.py:283
  794.2 10.4 fusion.33
  804.8 14.1 fusion.82
  818.9 21.1 convolution_add_fusion
  840.0 29.1 %gather_fusion.3 = f32[4096,1024]{1,0:T(8,128)} fusion(f32[5120,1024]{1,0:T(8,128)} %bitcast.277, s32[4096]{0:T(1024)S(1)} %copy-done.32), kind=kCustom, calls=%fused_computation.3 | custom fusion | bytes 33570816 | tf_op jit(solution)/shard_map/gather | solution.py:334
  869.1 8.2 bitcast_reduce_fusion
  883.9 92.8 %while.35 = (s32[]{:T(128)}, f32[8,512,128]{1,2,0:T(8,128)S(1)}, f32[8,512,64]{1,2,0:T(8,128)S(1)}, bf16[8,512,64]{1,2,0:T(8,128)(2,1)}, s32[8]{0:T(128)}, /*ind...) while((s32[]{:T(128)}, f32[8,512,128]{1,2,0:T(8,128)S(1)}, ...), condition=%wide.region_20.21_spmd.clone.clone, body=%wide.region_18.20_spmd.clone.sunk.clone | while | flops 340622336 | bytes 18830076 | solution.py:208
  984.5 4.5 convolution_convert_fusion.4
  997.3 17.6 convolution_convert_fusion
  1015.0 16.6 convolution_convert_fusion.2
  1031.7 17.5 convolution_convert_fusion.1
  1051.4 7.7 reduce-scatter.15.cloned.1.call-done
  1059.1 34.8 %reduce-scatter.9.cloned.1.call-done = bf16[512,1024]{1,0:T(8,128)(2,1)} async-done(((bf16[1024,1024]{1,0:T(8,128)(2,1)}), bf16[512,1024]{1,0:T(8,128)(2,1)}) %reduce-scatter.9.cloned.1.call-update) | async-done | bytes 1048592 | tf_op jit(solution)/shard_map/reduce_scatter | solution.py:400
  1093.9 191.9 %reduce-scatter.23.cloned.1.call-done = bf16[8,512,1024]{2,1,0:T(8,128)(2,1)} async-done(((bf16[16,512,1024]{2,1,0:T(8,128)(2,1)}), bf16[8,512,1024]{2,1,0:T(8,128)(2,1)}) %reduce-scatter.23.cloned.1.call-update) | async-done | bytes 8388624 | tf_op jit(solution)/shard_map/reduce_scatter | solution.py:329
  1285.8 192.1 %reduce-scatter.19.cloned.1.call-done = bf16[8,1024,512]{2,1,0:T(8,128)(2,1)} async-done(((bf16[16,1024,512]{2,1,0:T(8,128)(2,1)}), bf16[8,1024,512]{2,1,0:T(8,128)(2,1)}) %reduce-scatter.19.cloned.1.call-update) | async-done | bytes 8388624 | tf_op jit(solution)/shard_map/reduce_scatter | solution.py:323
  1477.9 191.9 %reduce-scatter.21.cloned.1.call-done = bf16[8,1024,512]{2,1,0:T(8,128)(2,1)} async-done(((bf16[16,1024,512]{2,1,0:T(8,128)(2,1)}), bf16[8,1024,512]{2,1,0:T(8,128)(2,1)}) %reduce-scatter.21.cloned.1.call-update) | async-done | bytes 8388624 | tf_op jit(solution)/shard_map/reduce_scatter | solution.py:326
  1675.0 3.6 fusion.44
  1678.6 4.9 all-reduce.6
  1683.7 4.1 fusion.41
  1687.8 63.8 %all-reduce.4 = (bf16[512]{0:T(512)(128)(2,1)S(1)}, bf16[512]{0:T(512)(128)(2,1)S(1)}, bf16[512,16]{0,1:T(8,128)(2,1)S(1)}) all-reduce(bf16[512]{0:T(512)(128)(2,1)S(1)} %dynamic-slice.1, bf16[512]{0:T(512)(128)(2,1)S(1)} %dynamic-slice.3, ...), channel_id=1, replica_groups=mesh['replica'=16,'group'=2] {'replica'}, use_global_device_ids=true, to_apply=%region_24.25 | all-reduce | flops 9216 | bytes 36864 | tf_op jit(solution)/shard_map/psum | solution.py:420
  1753.4 426.8 %all-reduce.9.cloned.1.call-done = (bf16[512,1024]{1,0:T(8,128)(2,1)}, bf16[512,512]{1,0:T(8,128)(2,1)}, bf16[512,512]{1,0:T(8,128)(2,1)}, bf16[512,1024]{1,0:T(...) async-done(((bf16[512,1024]{1,0:T(8,128)(2,1)}, bf16[512,512]{1,0:T(8,128)(2,1)}, ...) | async-done | bytes 28311568 | tf_op jit(solution)/shard_map/psum | solution.py:421
  2180.2 11.9 convert_element_type.250
  2192.1 11.9 convert_element_type.252
  2204.0 11.8 convert_element_type.254
  (398 shorter events, 191.0 us)
Async XLA Ops:
  7.2 48.1 %all-gather.12.cloned.1.call-start = ((), (), s32[]{:S(2)}) async-start(), calls=%async_computation.9 | async-start | bytes 1572864 | tf_op jit(solution)/shard_map/all_gather | solution.py:238
  7.9 50.3 %all-gather.10.cloned.1.call-start = ((), (), s32[]{:S(2)}) async-start(), calls=%async_computation.8 | async-start | bytes 1572864 | tf_op jit(solution)/shard_map/all_gather | solution.py:239
  8.7 83.0 %all-gather.14.cloned.1.call-start = ((), (), s32[]{:S(2)}) async-start(), calls=%async_computation.10 | async-start | bytes 3145728 | tf_op jit(solution)/shard_map/all_gather | solution.py:237
  9.4 154.4 %all-gather.16.cloned.1.call-start = ((), (), s32[]{:S(2)}) async-start(), calls=%async_computation.11 | async-start | bytes 3145728 | tf_op jit(solution)/shard_map/all_gather | solution.py:240
  10.0 316.5 %all-gather.18.cloned.1.call-start = ((), (), s32[]{:S(2)}) async-start(), calls=%async_computation.12 | async-start | bytes 25165824 | tf_op jit(solution)/shard_map/all_gather | solution.py:275
  10.6 516.2 %all-gather.20.cloned.1.call-start = ((), (), s32[]{:S(2)}) async-start(), calls=%async_computation.13 | async-start | bytes 25165824 | tf_op jit(solution)/shard_map/all_gather | solution.py:276
  11.1 1.9 copy-start.27
  11.1 716.1 %all-gather.22.cloned.1.call-start = ((), (), s32[]{:S(2)}) async-start(), calls=%async_computation.14 | async-start | bytes 25165824 | tf_op jit(solution)/shard_map/all_gather | solution.py:277
  11.9 1.6 copy-start.4
  11.9 2.5 copy-start.47
  11.9 1039.4 %reduce-scatter.11.cloned.1.call-start = ((), (), s32[]{:S(2)}) async-start(), calls=%async_computation.16 | async-start | bytes 1572864 | tf_op jit(solution)/shard_map/reduce_scatter | solution.py:403
  14.4 77.2 %copy-start.40 = (f32[512]{0:T(512)}, f32[512]{0:T(512)S(1)}, u32[]{:S(2)}) copy-start(f32[512]{0:T(512)S(1)} %get-tuple-element.470) | copy-start | bytes 6148
  19.7 72.0 %copy-start.35 = (f32[2,1,512]{2,1,0:T(1,128)}, f32[2,1,512]{2,1,0:T(1,128)S(1)}, u32[]{:S(2)}) copy-start(f32[2,1,512]{2,1,0:T(1,128)S(1)} %convert_element_type.256) | copy-start | bytes 12292
  20.0 81.2 %copy-start.13 = (f32[512,64]{0,1:T(8,128)}, f32[512,64]{0,1:T(8,128)S(1)}, u32[]{:S(2)}) copy-start(f32[512,64]{0,1:T(8,128)S(1)} %pad_maximum_fusion.2) | copy-start | bytes 393220
  20.1 37.9 %copy-start.15 = (f32[512,64]{0,1:T(8,128)}, f32[512,64]{0,1:T(8,128)S(1)}, u32[]{:S(2)}) copy-start(f32[512,64]{0,1:T(8,128)S(1)} %pad_maximum_fusion.1) | copy-start | bytes 393220
  20.3 1.8 copy-start.48
  20.3 6.2 copy-start.43
  26.5 141.7 %copy-start.33 = (f32[2,1,512]{2,1,0:T(1,128)}, f32[2,1,512]{2,1,0:T(1,128)S(1)}, u32[]{:S(2)}) copy-start(f32[2,1,512]{2,1,0:T(1,128)S(1)} %convert_element_type.257) | copy-start | bytes 12292
  31.3 137.9 %copy-start.30 = (bf16[1024,16]{0,1:T(8,128)(2,1)}, bf16[1024,16]{0,1:T(8,128)(2,1)S(1)}, u32[]{:S(2)}) copy-start(bf16[1024,16]{0,1:T(8,128)(2,1)S(1)} %all_gather.46) | copy-start | bytes 98308
  163.8 3.8 copy-start.17
  753.3 14.8 copy-start.32
  869.1 8.2 copy-start.1
  869.1 8.2 copy-start.31
  869.1 8.2 copy-start.34
  869.1 8.2 copy-start.39
  877.3 1.8 copy-start.11
  877.4 1.8 copy-start.45
  879.2 1.7 copy-start.18
  880.9 2.3 copy-start.6
  880.9 2.8 copy-start.8
  880.9 3.0 copy-start.12
  883.9 94.2 %copy-start.14 = (f32[512,64]{0,1:T(8,128)S(1)}, f32[512,64]{0,1:T(8,128)}, u32[]{:S(2)}) copy-start(f32[512,64]{0,1:T(8,128)} %copy-done.13) | copy-start | bytes 393220
  979.2 2.2 copy-start.19
  981.4 69.9 %reduce-scatter.13.cloned.1.call-start = ((), (), s32[]{:S(2)}) async-start(), calls=%async_computation.17 | async-start | bytes 1572864 | tf_op jit(solution)/shard_map/reduce_scatter | solution.py:406
  984.5 74.7 %reduce-scatter.15.cloned.1.call-start = ((), (), s32[]{:S(2)}) async-start(), calls=%async_computation.18 | async-start | bytes 3145728 | tf_op jit(solution)/shard_map/reduce_scatter | solution.py:409
  989.1 104.8 %reduce-scatter.9.cloned.1.call-start = ((), (), s32[]{:S(2)}) async-start(), calls=%async_computation.15 | async-start | bytes 3145728 | tf_op jit(solution)/shard_map/reduce_scatter | solution.py:400
  997.3 288.5 %reduce-scatter.23.cloned.1.call-start = ((), (), s32[]{:S(2)}) async-start(), calls=%async_computation.22 | async-start | bytes 25165824 | tf_op jit(solution)/shard_map/reduce_scatter | solution.py:329
  1014.9 463.0 %reduce-scatter.19.cloned.1.call-start = ((), (), s32[]{:S(2)}) async-start(), calls=%async_computation.20 | async-start | bytes 25165824 | tf_op jit(solution)/shard_map/reduce_scatter | solution.py:323
  1031.6 638.2 %reduce-scatter.21.cloned.1.call-start = ((), (), s32[]{:S(2)}) async-start(), calls=%async_computation.21 | async-start | bytes 25165824 | tf_op jit(solution)/shard_map/reduce_scatter | solution.py:326
  1049.2 638.6 %reduce-scatter.17.cloned.1.call-start = ((), (), s32[]{:S(2)}) async-start(), calls=%async_computation.19 | async-start | bytes 49152 | tf_op jit(solution)/shard_map/reduce_scatter | solution.py:415
  1051.3 1128.9 %all-reduce.9.cloned.1.call-start = ((), (), s32[]{:S(2)}) async-start(), calls=%async_computation.23 | async-start | bytes 56623104 | tf_op jit(solution)/shard_map/psum | solution.py:421
  1669.8 1.9 copy-start.20
  1669.8 1.9 copy-start.21
  1671.7 1.9 copy-start.49
  1675.0 3.6 copy-start.46
  1675.0 8.7 copy-start.44
  2204.0 11.8 copy-start.23
  2217.3 2.7 copy-start.28
  (19 other events, 23.3 us)
Sparse Core Ops, SparseCore 0:
  9.6 24.3 all-gather.11
  35.5 21.3 all-gather.9
  58.5 33.1 all-gather.13
  93.0 33.1 all-gather.15
  127.6 198.8 all-gather.17
  327.9 198.8 all-gather.19
  528.3 198.8 all-gather.21
  981.6 20.3 reduce-scatter.10
  1004.2 20.3 reduce-scatter.12
  1027.3 31.8 reduce-scatter.14
  1062.1 31.8 reduce-scatter.8
  1096.6 189.1 reduce-scatter.22
  1288.8 189.1 reduce-scatter.18
  1480.7 189.1 reduce-scatter.20
  1672.5 9.8 reduce-scatter.16
  1688.9 491.2 all-reduce.8
where the time goes:
time: 2240 us; the launch traced here: 2230 us
  waiting for transfers between devices  1500 us (67%)
  matrix products  258 us (12%)
  local copies, waits for them, and re-layouts  240 us (11%)
  other arithmetic  107 us (5%)
  blocking collectives  83.1 us (4%)
    psum x1, waiting for transfers between devices, shards(): lax.psum(query_own.astype(jnp.bfloat16), 'replica').astype(jnp.float32)  427 us
    reduce_scatter x1, waiting for transfers between devices, shards(): lax.psum_scatter(gate_whole.astype(jnp.bfloat16), 'group', scatter_dimens...  192 us
    reduce_scatter x1, waiting for transfers between devices, shards(): lax.psum_scatter(up_whole.astype(jnp.bfloat16), 'group', scatter_dimensio...  192 us
    reduce_scatter x1, waiting for transfers between devices, shards(): lax.psum_scatter(down_whole.astype(jnp.bfloat16), 'group', scatter_dimens...  192 us
    all_gather x1, waiting for transfers between devices, shards(): up_part = lax.all_gather(up_weight, 'group', axis=0, tiled=True)  184 us
    all_gather x1, waiting for transfers between devices, shards(): down_part = lax.all_gather(down_weight, 'group', axis=0, tiled=True)  184 us
    psum x1, blocking collectives, shards(): lax.psum(gain_one_own.astype(jnp.bfloat16), 'replica').astype(jnp.float32)  63.8 us
    all_gather x1, waiting for transfers between devices, shards(): gate_part = lax.all_gather(gate_weight, 'group', axis=0, tiled=True)  56.5 us
  transfers between devices with their start and end apart: 16, of which 10 were waited for; matrix products, arithmetic and copies ran while one was open for 14% of the time, Pallas kernels for 0%

commit v1 on v0

v1 whole, which is shorter than its diff:
```python
import functools

import jax
import jax.numpy as jnp
from jax import lax
from jax.sharding import PartitionSpec as P

HQ = 16
KV = 8
HD = 64
E = 16
GRP = 2


norm_eps = 1e-06
residual_scale = 0.22
score_scale = 0.015625
rope_base = 10000.0
masked_value = -1e30


def rope_tables(length):
    positions = jnp.arange(length, dtype=jnp.float32)
    inverse = rope_base ** (-jnp.arange(0, HD, 2, dtype=jnp.float32) / HD)
    angles = positions[:, None] * inverse[None, :]
    cosine_table = jnp.cos(angles)
    sine_table = jnp.sin(angles)
    return (
        jnp.concatenate([cosine_table, cosine_table], -1),
        jnp.concatenate([sine_table, sine_table], -1),
    )


def rotate(values, cosine_table, sine_table):
    half_width = values.shape[-1] // 2
    turned = jnp.concatenate([-values[..., half_width:], values[..., :half_width]], -1)
    return values * cosine_table[:, None, :] + turned * sine_table[:, None, :]


def rotate_back(grads, cosine_table, sine_table):
    half_width = grads.shape[-1] // 2
    with_sine = grads * sine_table[:, None, :]
    turned = jnp.concatenate([with_sine[..., half_width:], -with_sine[..., :half_width]], -1)
    return grads * cosine_table[:, None, :] + turned


def swap(values, axis, size, bit):
    return lax.ppermute(values, axis, [(i, i ^ bit) for i in range(size)])


def side_of(axis, bit):
    return (lax.axis_index(axis) // bit) % 2


def bits_of(size):
    return [1 << place for place in range(size.bit_length() - 1)]


def fold(values, dim, axis, size, bit):
    side = side_of(axis, bit)
    half = values.shape[dim] // 2
    send = lax.dynamic_slice_in_dim(values, (1 - side) * half, half, dim)
    keep = lax.dynamic_slice_in_dim(values, side * half, half, dim)
    received = swap(send, axis, size, bit)
    return (keep.astype(jnp.float32) + received.astype(jnp.float32)).astype(jnp.bfloat16)


def unfold(values, dim, axis, size, bit, kept=jnp.bfloat16):
    side = side_of(axis, bit)
    other = swap(values, axis, size, bit).astype(kept)
    values = values.astype(kept)
    lower = jnp.where(side == 0, values, other)
    upper = jnp.where(side == 0, other, values)
    return jnp.concatenate([lower, upper], dim)


def group_gather(values, groups):
    for bit in bits_of(groups):
        values = unfold(values, 0, "group", groups, bit, values.dtype)
    return values


def group_scatter(values, groups):
    for bit in reversed(bits_of(groups)):
        values = fold(values, 0, "group", groups, bit)
    return values


def gather_rows(values, replicas, groups):
    rows, columns = values.shape
    half = rows // 2
    part = lax.dynamic_slice_in_dim(values, side_of("replica", 1) * half, half, 0)
    part = group_gather(part[None], groups)
    return unfold(part, 1, "replica", replicas, 1).reshape(groups * rows, columns)


def replica_sum(values, replicas, dim):
    for bit in bits_of(replicas):
        values = fold(values, dim, "replica", replicas, bit)
    for bit in reversed(bits_of(replicas)):
        kept = jnp.float32 if bit == 1 else jnp.bfloat16
        values = unfold(values, dim, "replica", replicas, bit, kept)
    return values


def own_rows_sum(values, replicas, groups):
    rows, columns = values.shape
    values = values.astype(jnp.bfloat16).reshape(groups, rows // groups, columns)
    values = fold(values, 1, "replica", replicas, 1)
    values = group_scatter(values, groups)
    for bit in bits_of(replicas)[1:]:
        values = fold(values, 1, "replica", replicas, bit)
    for bit in reversed(bits_of(replicas)):
        values = unfold(values, 1, "replica", replicas, bit)
    return values[0].astype(jnp.float32)


def expert_sum(values, replicas):
    shape = values.shape
    flat = values.astype(jnp.bfloat16).reshape(shape[0] * shape[1], shape[2])
    return replica_sum(flat, replicas, 0).reshape(shape)


def head_slices(queries, key_rows, values, group_index, length):
    query_block = lax.dynamic_slice_in_dim(queries, group_index * GRP * HD, GRP * HD, 1).reshape(
        length, GRP, HD
    )
    key_block = lax.dynamic_slice_in_dim(key_rows, group_index * HD, HD, 1)
    value_block = lax.dynamic_slice_in_dim(values, group_index * HD, HD, 1)
    return (query_block, key_block, value_block)


def attend_forward(queries, key_rows, values, causal):
    length = queries.shape[0]

    def one_group(group_index):
        query_block, key_block, value_block = head_slices(
            queries, key_rows, values, group_index, length
        )
        scores = (
            jnp.einsum("sgd,td->gst", query_block, key_block, preferred_element_type=jnp.float32)
            * score_scale
        )
        scores = jnp.where(causal[None], scores, masked_value)
        row_peak = jnp.max(scores, axis=-1, keepdims=True)
        exponent = jnp.exp(scores - row_peak)
        row_total = jnp.sum(exponent, axis=-1, keepdims=True)
        probability = (exponent / row_total).astype(jnp.bfloat16)
        block_mix = jnp.einsum(
            "gst,td->sgd", probability, value_block, preferred_element_type=jnp.float32
        )
        return (block_mix.reshape(length, GRP * HD), (row_peak + jnp.log(row_total))[..., 0])

    blocks, log_sums = lax.map(one_group, jnp.arange(KV, dtype=jnp.int32))
    return (blocks.transpose(1, 0, 2).reshape(length, HQ * HD), log_sums)


def attend_backward(queries, key_rows, values, grad_mix, log_sums, causal):
    length = queries.shape[0]

    def one_group(paired):
        group_index, group_sums = paired
        query_block, key_block, value_block = head_slices(
            queries, key_rows, values, group_index, length
        )
        grad_block = lax.dynamic_slice_in_dim(
            grad_mix, group_index * GRP * HD, GRP * HD, 1
        ).reshape(length, GRP, HD)
        scores = (
            jnp.einsum("sgd,td->gst", query_block, key_block, preferred_element_type=jnp.float32)
            * score_scale
        )
        scores = jnp.where(causal[None], scores, masked_value)
        probability = jnp.exp(scores - group_sums[..., None])
        rounded = probability.astype(jnp.bfloat16)
        grad_prob = jnp.einsum(
            "sgd,td->gst", grad_block, value_block, preferred_element_type=jnp.float32
        )
        grad_scores = probability * (
            grad_prob - jnp.sum(probability * grad_prob, axis=-1, keepdims=True)
        )
        grad_scores = grad_scores.astype(jnp.bfloat16)
        grad_query = (
            jnp.einsum("gst,td->sgd", grad_scores, key_block, preferred_element_type=jnp.float32)
            * score_scale
        )
        grad_key = (
            jnp.einsum("gst,sgd->td", grad_scores, query_block, preferred_element_type=jnp.float32)
            * score_scale
        )
        grad_value = jnp.einsum(
            "gst,sgd->td", rounded, grad_block, preferred_element_type=jnp.float32
        )
        return (grad_query.reshape(length, GRP * HD), grad_key, grad_value)

    query_parts, key_parts, value_parts = lax.map(
        one_group, (jnp.arange(KV, dtype=jnp.int32), log_sums)
    )
    return (
        query_parts.transpose(1, 0, 2).reshape(length, HQ * HD),
        key_parts.transpose(1, 0, 2).reshape(length, KV * HD),
        value_parts.transpose(1, 0, 2).reshape(length, KV * HD),
    )


def shards(
    replicas,
    groups,
    tokens,
    cotangent,
    routes,
    first_gain,
    query_weight,
    key_weight,
    value_weight,
    output_weight,
    second_gain,
    router_weight,
    gate_weight,
    up_weight,
    down_weight,
):
    length = tokens.shape[0]
    local_experts = gate_weight.shape[0]
    query_width = query_weight.shape[1]
    key_width = key_weight.shape[1]
    spare = 128 - E - 2
    wide = jnp.concatenate([query_weight, key_weight, value_weight], 1)
    late = jnp.concatenate(
        [
            output_weight,
            router_weight,
            second_gain[:, None],
            first_gain[:, None],
            jnp.zeros((output_weight.shape[0], spare), jnp.bfloat16),
        ],
        1,
    )
    gain_one = group_gather(first_gain, groups)
    wide_full = gather_rows(wide, replicas, groups)
    late_full = gather_rows(late, replicas, groups)
    routes_all = group_gather(routes, groups)
    cotangent_all = group_gather(cotangent, groups)
    output_width = output_weight.shape[1]
    output_full = late_full[:, :output_width]
    router_full = late_full[:, output_width : output_width + E]
    gain_two = late_full[:, output_width + E]
    tokens_float = tokens.astype(jnp.float32)
    scale_one = lax.rsqrt(jnp.mean(tokens_float * tokens_float, axis=-1, keepdims=True) + norm_eps)
    normed_one = (tokens_float * scale_one * gain_one.astype(jnp.float32)).astype(jnp.bfloat16)
    cosine_table, sine_table = rope_tables(length)
    projected = jnp.dot(normed_one, wide_full, preferred_element_type=jnp.float32)
    query_pre = projected[:, :query_width].reshape(length, HQ, HD)
    queries = (
        rotate(query_pre, cosine_table, sine_table).astype(jnp.bfloat16).reshape(length, HQ * HD)
    )
    key_pre = projected[:, query_width : query_width + key_width].reshape(length, KV, HD)
    key_rows = (
        rotate(key_pre, cosine_table, sine_table).astype(jnp.bfloat16).reshape(length, KV * HD)
    )
    values = projected[:, query_width + key_width :].astype(jnp.bfloat16)
    causal = jnp.arange(length)[:, None] >= jnp.arange(length)[None, :]
    attention_raw, log_sums = attend_forward(queries, key_rows, values, causal)
    attention_mix = attention_raw.astype(jnp.bfloat16)
    attention_out = jnp.dot(attention_mix, output_full, preferred_element_type=jnp.float32)
    resid = tokens_float + residual_scale * attention_out
    scale_two = lax.rsqrt(jnp.mean(resid * resid, axis=-1, keepdims=True) + norm_eps)
    normed_two = (resid * scale_two * gain_two.astype(jnp.float32)).astype(jnp.bfloat16)

    normed_all = group_gather(normed_two, groups)
    logits = jnp.dot(normed_all, router_full, preferred_element_type=jnp.float32)
    chosen = jnp.any(
        routes_all[:, :, None] == jnp.arange(E, dtype=jnp.int32)[None, None, :], axis=1
    )
    shown = jnp.where(chosen, logits, -jnp.inf)
    gates = jax.nn.softmax(shown, axis=-1)
    first_expert = lax.axis_index("group") * local_experts
    gates_local = lax.dynamic_slice_in_dim(gates, first_expert, local_experts, 1)
    gates_column = gates_local.T[:, :, None]

    gate_pre = jnp.einsum(
        "td,edf->etf", normed_all, gate_weight, preferred_element_type=jnp.float32
    )
    up_pre = jnp.einsum("td,edf->etf", normed_all, up_weight, preferred_element_type=jnp.float32)
    sigmoid_gate = jax.nn.sigmoid(gate_pre)
    swish_gate = gate_pre * sigmoid_gate
    hidden = swish_gate * up_pre
    hidden_gated = (gates_column * hidden).astype(jnp.bfloat16)
    grad_hidden_plain = residual_scale * jnp.einsum(
        "td,efd->etf", cotangent_all, down_weight, preferred_element_type=jnp.float32
    )
    down_part = residual_scale * jnp.einsum(
        "etf,td->efd", hidden_gated, cotangent_all, preferred_element_type=jnp.float32
    )
    down_grad = expert_sum(down_part, replicas)
    grad_gates = jnp.sum(grad_hidden_plain * hidden, axis=-1).T
    grad_hidden = gates_column * grad_hidden_plain
    grad_gate = (
        grad_hidden * up_pre * sigmoid_gate * (1.0 + gate_pre * (1.0 - sigmoid_gate))
    ).astype(jnp.bfloat16)
    grad_up = (grad_hidden * swish_gate).astype(jnp.bfloat16)
    gate_part = jnp.einsum(
        "td,etf->edf", normed_all, grad_gate, preferred_element_type=jnp.float32
    )
    gate_grad = expert_sum(gate_part, replicas)
    up_part = jnp.einsum("td,etf->edf", normed_all, grad_up, preferred_element_type=jnp.float32)
    up_grad = expert_sum(up_part, replicas)
    moe_part = jnp.einsum(
        "etf,efd->td", hidden_gated, down_weight, preferred_element_type=jnp.float32
    )
    moe_out = group_scatter(moe_part.astype(jnp.bfloat16), groups).astype(jnp.float32)
    layer_output = (resid + residual_scale * moe_out).astype(jnp.bfloat16)

    grad_chosen = gates_local * grad_gates
    grad_logits = lax.dynamic_update_slice_in_dim(
        jnp.zeros_like(gates), grad_chosen, first_expert, 1
    ) - gates * jnp.sum(grad_chosen, axis=-1, keepdims=True)
    grad_logits = grad_logits.astype(jnp.bfloat16)
    router_part = jnp.einsum(
        "sd,se->de", normed_all, grad_logits, preferred_element_type=jnp.float32
    )
    grad_normed_part = (
        jnp.einsum("etf,edf->td", grad_gate, gate_weight, preferred_element_type=jnp.float32)
        + jnp.einsum("etf,edf->td", grad_up, up_weight, preferred_element_type=jnp.float32)
        + jnp.einsum("se,de->sd", grad_logits, router_full, preferred_element_type=jnp.float32)
    )
    grad_normed_two = group_scatter(grad_normed_part.astype(jnp.bfloat16), groups).astype(
        jnp.float32
    )
    grad_out = cotangent.astype(jnp.float32)
    second_part = jnp.sum(grad_normed_two * resid * scale_two, axis=0)
    weighted_two = grad_normed_two * gain_two.astype(jnp.float32)
    grad_resid = (
        grad_out
        + scale_two * weighted_two
        - resid * scale_two**3 * jnp.mean(weighted_two * resid, axis=-1, keepdims=True)
    )
    grad_attention = (residual_scale * grad_resid).astype(jnp.bfloat16)
    output_part = jnp.einsum(
        "sk,sd->kd", attention_mix, grad_attention, preferred_element_type=jnp.float32
    )
    early_sum = own_rows_sum(
        jnp.concatenate(
            [
                output_part,
                router_part,
                second_part[:, None],
                jnp.zeros((output_part.shape[0], spare + 1), jnp.float32),
            ],
            1,
        ),
        replicas,
        groups,
    )
    grad_mix = jnp.einsum(
        "sd,kd->sk", grad_attention, output_full, preferred_element_type=jnp.float32
    ).astype(jnp.bfloat16)
    grad_query_rot, grad_key_rot, grad_value_raw = attend_backward(
        queries, key_rows, values, grad_mix, log_sums, causal
    )
    grad_query_pre = rotate_back(grad_query_rot.reshape(length, HQ, HD), cosine_table, sine_table)
    grad_key_pre = rotate_back(grad_key_rot.reshape(length, KV, HD), cosine_table, sine_table)
    grad_wide = jnp.concatenate(
        [
            grad_query_pre.reshape(length, HQ * HD).astype(jnp.bfloat16),
            grad_key_pre.reshape(length, KV * HD).astype(jnp.bfloat16),
            grad_value_raw.astype(jnp.bfloat16),
        ],
        1,
    )
    grad_normed_one = jnp.einsum(
        "sk,dk->sd", grad_wide, wide_full, preferred_element_type=jnp.float32
    )
    first_part = jnp.sum(grad_normed_one * tokens_float * scale_one, axis=0)
    wide_part = jnp.einsum("sd,sk->dk", normed_one, grad_wide, preferred_element_type=jnp.float32)
    late_sum = own_rows_sum(
        jnp.concatenate(
            [
                wide_part,
                first_part[:, None],
                jnp.zeros((wide_part.shape[0], 127), jnp.float32),
            ],
            1,
        ),
        replicas,
        groups,
    )
    weighted_one = grad_normed_one * gain_one.astype(jnp.float32)
    tokens_grad = (
        grad_resid
        + scale_one * weighted_one
        - tokens_float
        * scale_one**3
        * jnp.mean(weighted_one * tokens_float, axis=-1, keepdims=True)
    )
    wide_width = wide.shape[1]
    return (
        layer_output,
        tokens_grad,
        late_sum[:, wide_width],
        late_sum[:, :query_width],
        late_sum[:, query_width : query_width + key_width],
        late_sum[:, query_width + key_width : wide_width],
        early_sum[:, :output_width],
        early_sum[:, output_width + E],
        early_sum[:, output_width : output_width + E],
        gate_grad,
        up_grad,
        down_grad,
    )


def solution(mesh):
    return jax.shard_map(
        functools.partial(shards, mesh.shape["replica"], mesh.shape["group"]),
        mesh=mesh,
        in_specs=(
            P(("replica", "group"), None),
            P(("replica", "group"), None),
            P(("replica", "group"), None),
            P("group"),
            P("group", None),
            P("group", None),
            P("group", None),
            P("group", None),
            P("group"),
            P("group", None),
            P("group", None, None),
            P("group", None, None),
            P("group", None, None),
        ),
        out_specs=(
            P(("replica", "group"), None),
            P(("replica", "group"), None),
            P("group"),
            P("group", None),
            P("group", None),
            P("group", None),
            P("group", None),
            P("group"),
            P("group", None),
            P("group", None, None),
            P("group", None, None),
            P("group", None, None),
        ),
        check_vma=False,
    )
```

time: 2240 us -> 1040 us (0.46)
  waiting for transfers between devices: 1500 us -> 430 us
  local copies, waits for them, and re-layouts: 240 us -> 148 us
  blocking collectives: 83.1 us -> 0 us
  starting transfers between devices: 0.64 us -> 53.8 us
  matrix products: 258 us -> 232 us
  other arithmetic: 107 us -> 133 us
    reduce_scatter x8 -> x0, waiting for transfers between devices: 618 us -> none  [the longest x1 192 us: shards(): lax.psum_scatter(gate_whole.astype(jnp.bfloat16), 'group', scatter_dimens...]
    all_gather x7 -> x0, waiting for transfers between devices: 452 us -> none  [the longest x1 184 us: shards(): up_part = lax.all_gather(up_weight, 'group', axis=0, tiled=True)]
    ppermute x0 -> x52, waiting for transfers between devices: none -> 430 us  [swap(): return lax.ppermute(values, axis, [(i, i ^ bit) for i in range(size)])]
    psum x1 -> x0, waiting for transfers between devices: 427 us -> none  [shards(): lax.psum(query_own.astype(jnp.bfloat16), 'replica').astype(jnp.float32)]
    gather x9 -> x0, local copies, waits for them, and re-layouts: 142 us -> none  [the longest x5 33.6 us: shards(): jnp.take_along_axis(logits, routes, axis=1)]
    psum x1 -> x0, blocking collectives: 63.8 us -> none  [shards(): lax.psum(gain_one_own.astype(jnp.bfloat16), 'replica').astype(jnp.float32)]
    ppermute x0 -> x52, starting transfers between devices: none -> 53.8 us  [swap(): return lax.ppermute(values, axis, [(i, i ^ bit) for i in range(size)])]
    concatenate x0 -> x23, other arithmetic: none -> 35.5 us  [unfold(): return jnp.concatenate([lower, upper], dim)]
  transfers between devices with their start and end apart: 16 -> 52, of which waited for: 10 -> 26; matrix products, arithmetic and copies ran while one was open for 14% -> 34% of each run, Pallas kernels for 0% -> 0%
where the time goes in v1:
time: 1040 us; the launch traced here: 1020 us
  waiting for transfers between devices  430 us (41%)
  matrix products  232 us (22%)
  local copies, waits for them, and re-layouts  148 us (14%)
  other arithmetic  133 us (13%)
  starting transfers between devices  53.8 us (5%)
  loops' own time  21.7 us (2%)
    ppermute x52, waiting for transfers between devices, swap(): return lax.ppermute(values, axis, [(i, i ^ bit) for i in range(size)])  430 us
    ppermute x52, starting transfers between devices, swap(): return lax.ppermute(values, axis, [(i, i ^ bit) for i in range(size)])  53.8 us
    concatenate x23, other arithmetic, unfold(): return jnp.concatenate([lower, upper], dim)  35.5 us
    select_n x28, other arithmetic, unfold(): lower = jnp.where(side == 0, values, other)  33.1 us
    dot_general x1, matrix products, shards(): jnp.einsum('td,efd->etf', cotangent_all, down_weight, preferred_element_t...  29 us
    dot_general x16, matrix products, one_group(): jnp.einsum('sgd,td->gst', query_block, key_block, preferred_element_type=...  25.2 us
    convert_element_type x22, other arithmetic, fold(): (keep.astype(jnp.float32) + received.astype(jnp.float32)).astype(jnp.bflo...  22.8 us
    convert_element_type x2, local copies, waits for them, and re-layouts, expert_sum(): flat = values.astype(jnp.bfloat16).reshape(shape[0] * shape[1], shape[2])  22.7 us
  transfers between devices with their start and end apart: 52, of which 26 were waited for; matrix products, arithmetic and copies ran while one was open for 34% of the time, Pallas kernels for 0%

profile of v1, /device:TPU:0, one launch (start us, length us, event | category | flops | bytes accessed | tf_op | source)
XLA Modules:
  0.0 1021.8 jit_solution(5790156283618054825)
XLA Ops:
  14.5 10.9 %collective-permute-done.3 = bf16[1,256,1152]{2,1,0:T(8,128)(2,1)} collective-permute-done((bf16[1,256,1152]{2,1,0:T(8,128)(2,1)S(1)}, bf16[1,256,1152]{2,1,0:T(8,128)(2,1)}, u32[]{:S(2)}, u32[]{:S(2)}) %collective-permute-start.3) | collective-permute-done | bytes 589856 | tf_op jit(solution)/shard_map/ppermute | solution.py:48
  27.7 20.1 %collective-permute-done.1 = bf16[1,256,2048]{2,1,0:T(8,128)(2,1)} collective-permute-done((bf16[1,256,2048]{2,1,0:T(8,128)(2,1)}, bf16[1,256,2048]{2,1,0:T(8,128)(2,1)}, u32[]{:S(2)}, u32[]{:S(2)}) %collective-permute-start.1) | collective-permute-done | bytes 1048608 | tf_op jit(solution)/shard_map/ppermute | solution.py:48
  66.7 4.4 fusion.86
  97.4 50.9 %while.34 = (s32[]{:T(128)}, bf16[8,512,128]{1,2,0:T(8,128)(2,1)}, f32[8,2,512]{2,1,0:T(2,128)}, s32[8]{0:T(128)S(1)}, bf16[512,512]{0,1:T(8,128)(2,1)}, /*index...) while((s32[]{:T(128)}, bf16[8,512,128]{1,2,0:T(8,128)(2,1)}, ...), condition=%wide.region_4.5_spmd.clone.clone, body=%wide.region_1.4_spmd.clone.sunk.clone | while | flops 138673152 | bytes 7766241 | solution.py:154
  156.5 24.1 %collective-permute-done.5 = s32[512,8]{0,1:T(8,128)S(1)} collective-permute-done((s32[512,8]{0,1:T(8,128)S(1)}, s32[512,8]{0,1:T(8,128)S(1)}, u32[]{:S(2)}, u32[]{:S(2)}) %collective-permute-start.5) | collective-permute-done | bytes 16416 | tf_op jit(solution)/shard_map/ppermute | solution.py:48
  185.3 15.6 %fusion.63 = f32[1024,8,512]{0,2,1:T(8,128)} fusion(bf16[8,1024,512]{2,1,0:T(8,128)(2,1)} %param.28, bf16[512,1024]{1,0:T(8,128)(2,1)S(1)} %get-tuple-element.494, bf16[512,1024]{1,0:T(8,128)(2,1)S(1)} %get-tuple-element.493), kind=kOutput, calls=%fused_computation.139 | convolution fusion | flops 8594128896 | bytes 27262976 | tf_op jit(solution)/shard_map/td,edf->etf/dot_general | solution.py:284
  200.9 11.9 %fusion.65 = f32[1024,8,512]{0,2,1:T(8,128)} fusion(bf16[8,1024,512]{2,1,0:T(8,128)(2,1)S(1)} %bitcast.373, bf16[512,1024]{1,0:T(8,128)(2,1)S(1)} %get-tuple-element.494, bf16[512,1024]{1,0:T(8,128)(2,1)S(1)} %get-tuple-element.493), kind=kOutput, calls=%fused_computation.141 | convolution fusion | flops 8594128896 | bytes 27262976 | tf_op jit(solution)/shard_map/td,edf->etf/dot_general | solution.py:281
  214.6 29.0 %fusion.33 = (f32[8,1024]{1,0:T(8,128)S(1)}, bf16[8,1024,512]{1,2,0:T(8,128)(2,1)}, bf16[8,1024,512]{1,2,0:T(8,128)(2,1)}, bf16[8,1024,512]{1,2,0:T(8,128)(2,1)}) fusion(f32[1024,8,512]{0,2,1:T(8,128)} %fusion.63, f32[1024,8,512]{0,2,1:T(8,128)} %fusion.65, f32[8,1024]{1,0:T(8,128)S(1)} %get-tuple-element.451, f32[8,1024]{1,0:T(8,128)S(1)} %get-tuple-element.452, ...), kind=kOutput, calls=%fused_computation.54 | convolution fusion | flops 8678006784 | bytes 69304320 | tf_op jit(solution)/shard_map/td,efd->etf/dot_general | solution.py:289
  243.5 12.8 %fusion.106 = f32[1024,1024,1]{1,0,2:T(8,128)S(1)} fusion(bf16[8,1024,512]{1,2,0:T(8,128)(2,1)} %get-tuple-element.458, bf16[8,1024,512]{2,1,0:T(8,128)(2,1)} %param.27), kind=kOutput, calls=%fused_computation.318 | convolution fusion | flops 8589934592 | bytes 20971520 | tf_op jit(solution)/shard_map/etf,edf->td/dot_general | solution.py:323
  256.4 14.8 %convert_bitcast_fusion.1 = bf16[8,1024,512]{1,2,0:T(8,128)(2,1)} fusion(bf16[8,1024,512]{1,2,0:T(8,128)(2,1)} %get-tuple-element.458, bf16[512,1024]{1,0:T(8,128)(2,1)S(1)} %copy-done.48, bf16[512,1024]{1,0:T(8,128)(2,1)S(1)} %copy-done.45), kind=kOutput, calls=%fused_computation.80 | convolution fusion | flops 8598323200 | bytes 18874368 | tf_op jit(solution)/shard_map/td,etf->edf/dot_general | solution.py:302
  271.2 12.8 %fusion.107 = f32[1024,1024,1]{1,0,2:T(8,128)S(1)} fusion(bf16[8,1024,512]{1,2,0:T(8,128)(2,1)} %get-tuple-element.459, bf16[8,1024,512]{2,1,0:T(8,128)(2,1)} %param.28), kind=kOutput, calls=%fused_computation.319 | convolution fusion | flops 8589934592 | bytes 20971520 | tf_op jit(solution)/shard_map/etf,edf->td/dot_general | solution.py:324
  284.1 14.7 %convert_bitcast_fusion = bf16[8,1024,512]{1,2,0:T(8,128)(2,1)} fusion(bf16[8,1024,512]{1,2,0:T(8,128)(2,1)} %get-tuple-element.459, bf16[512,1024]{1,0:T(8,128)(2,1)S(1)} %copy-done.48, bf16[512,1024]{1,0:T(8,128)(2,1)S(1)} %copy-done.45), kind=kOutput, calls=%fused_computation.78 | convolution fusion | flops 8598323200 | bytes 18874368 | tf_op jit(solution)/shard_map/td,etf->edf/dot_general | solution.py:306
  298.8 11.2 %bitcast_convert_fusion = bf16[1024,1024]{1,0:T(8,128)(2,1)S(1)} fusion(bf16[8,1024,512]{1,2,0:T(8,128)(2,1)} %get-tuple-element.460, bf16[8,512,1024]{2,1,0:T(8,128)(2,1)S(1)} %bitcast.375), kind=kOutput, calls=%fused_computation.95 | convolution fusion | flops 8590983168 | bytes 18874368 | tf_op jit(solution)/shard_map/etf,efd->td/dot_general | solution.py:308
  310.0 15.8 %multiply_convert_fusion = bf16[8,512,1024]{2,1,0:T(8,128)(2,1)} fusion(bf16[8,1024,512]{1,2,0:T(8,128)(2,1)} %get-tuple-element.460, bf16[512,1024]{1,0:T(8,128)(2,1)S(1)} %copy-done.41, bf16[512,1024]{1,0:T(8,128)(2,1)S(1)} %get-tuple-element.491), kind=kOutput, calls=%fused_computation.67 | convolution fusion | flops 8602517504 | bytes 18874368 | tf_op jit(solution)/shard_map/etf,td->efd/dot_general | solution.py:292
  331.8 11.4 %copy.157 = bf16[8,1024,512]{2,1,0:T(8,128)(2,1)} copy(bf16[8,1024,512]{1,2,0:T(8,128)(2,1)} %convert_bitcast_fusion.1) | data formatting | bytes 16777216 | tf_op jit(solution)/shard_map/convert_element_type | solution.py:120
  343.1 4.7 constant_dynamic-slice_fusion.14
  349.0 11.4 %copy.158 = bf16[8,1024,512]{2,1,0:T(8,128)(2,1)} copy(bf16[8,1024,512]{1,2,0:T(8,128)(2,1)} %convert_bitcast_fusion) | data formatting | bytes 16777216 | tf_op jit(solution)/shard_map/convert_element_type | solution.py:120
  360.4 4.5 constant_dynamic-slice_fusion.10
  365.4 4.7 constant_dynamic-slice_fusion.6
  381.9 92.9 %while.35 = (s32[]{:T(128)}, f32[8,512,128]{1,2,0:T(8,128)}, f32[8,512,64]{1,2,0:T(8,128)S(1)}, bf16[8,512,64]{1,2,0:T(8,128)(2,1)}, s32[8]{0:T(128)S(1)}, /*ind...) while((s32[]{:T(128)}, f32[8,512,128]{1,2,0:T(8,128)}, ...), condition=%wide.region_14.15_spmd.clone.clone, body=%wide.region_12.14_spmd.clone.sunk.clone | while | flops 340622336 | bytes 18829576 | solution.py:196
  482.6 4.1 concatenate.162
  498.4 7.9 collective-permute-done.20
  509.1 5.7 convolution_convert_fusion
  514.9 7.9 concatenate.155
  546.9 4.6 collective-permute-done.26
  552.6 4.1 add_convert_fusion.2
  558.7 10.2 collective-permute-done.11
  576.3 42.5 %collective-permute-done.12 = bf16[1,128,2176]{2,1,0:T(8,128)(2,1)S(1)} collective-permute-done((bf16[1,128,2176]{2,1,0:T(8,128)(2,1)S(1)}, bf16[1,128,2176]{2,1,0:T(8,128)(2,1)S(1)}, u32[]{:S(2)}, u32[]{:S(2)}) %collective-permute-start.12) | collective-permute-done | bytes 557088 | tf_op jit(solution)/shard_map/ppermute | solution.py:48
  621.1 5.6 add_convert_fusion
  636.2 4.2 collective-permute-done.15
  640.5 4.7 collective-permute-start.16
  647.6 16.1 %collective-permute-done.37 = bf16[2048,512]{1,0:T(8,128)(2,1)S(1)} collective-permute-done((bf16[2048,512]{1,0:T(8,128)(2,1)S(1)}, bf16[2048,512]{1,0:T(8,128)(2,1)S(1)}, u32[]{:S(2)}, u32[]{:S(2)}) %collective-permute-start.37) | collective-permute-done | bytes 2097184 | tf_op jit(solution)/shard_map/ppermute | solution.py:48
  666.6 41.0 %collective-permute-done.45 = bf16[1024,1024]{1,0:T(8,128)(2,1)S(1)} collective-permute-done((bf16[1024,1024]{1,0:T(8,128)(2,1)S(1)}, bf16[1024,1024]{1,0:T(8,128)(2,1)S(1)}, u32[]{:S(2)}, u32[]{:S(2)}) %collective-permute-start.45) | collective-permute-done | bytes 2097184 | tf_op jit(solution)/shard_map/ppermute | solution.py:48
  714.8 29.0 %collective-permute-done.31 = bf16[512,512]{1,0:T(8,128)(2,1)S(1)} collective-permute-done((bf16[512,512]{1,0:T(8,128)(2,1)S(1)}, bf16[512,512]{1,0:T(8,128)(2,1)S(1)}, u32[]{:S(2)}, u32[]{:S(2)}) %collective-permute-start.31) | collective-permute-done | bytes 524320 | tf_op jit(solution)/shard_map/ppermute | solution.py:48
  751.0 43.1 %collective-permute-done.32 = bf16[512,512]{1,0:T(8,128)(2,1)S(1)} collective-permute-done((bf16[512,512]{1,0:T(8,128)(2,1)S(1)}, bf16[512,512]{1,0:T(8,128)(2,1)S(1)}, u32[]{:S(2)}, u32[]{:S(2)}) %collective-permute-start.32) | collective-permute-done | bytes 524320 | tf_op jit(solution)/shard_map/ppermute | solution.py:48
  794.4 10.9 %collective-permute-done.39 = bf16[512,512]{1,0:T(8,128)(2,1)S(1)} collective-permute-done((bf16[512,512]{1,0:T(8,128)(2,1)S(1)}, bf16[512,512]{1,0:T(8,128)(2,1)S(1)}, u32[]{:S(2)}, u32[]{:S(2)}) %collective-permute-start.39) | collective-permute-done | bytes 524320 | tf_op jit(solution)/shard_map/ppermute | solution.py:48
  806.2 11.6 %collective-permute-done.47 = bf16[256,1024]{1,0:T(8,128)(2,1)S(1)} collective-permute-done((bf16[256,1024]{1,0:T(8,128)(2,1)S(1)}, bf16[256,1024]{1,0:T(8,128)(2,1)S(1)}, u32[]{:S(2)}, u32[]{:S(2)}) %collective-permute-start.47) | collective-permute-done | bytes 524320 | tf_op jit(solution)/shard_map/ppermute | solution.py:48
  818.1 32.2 %collective-permute-done.40 = bf16[512,512]{1,0:T(8,128)(2,1)S(1)} collective-permute-done((bf16[512,512]{1,0:T(8,128)(2,1)S(1)}, bf16[512,512]{1,0:T(8,128)(2,1)S(1)}, u32[]{:S(2)}, u32[]{:S(2)}) %collective-permute-start.40) | collective-permute-done | bytes 524320 | tf_op jit(solution)/shard_map/ppermute | solution.py:48
  853.1 6.4 collective-permute-done.48
  860.8 21.2 %collective-permute-done.41 = bf16[1024,512]{1,0:T(8,128)(2,1)S(1)} collective-permute-done((bf16[1024,512]{1,0:T(8,128)(2,1)S(1)}, bf16[1024,512]{1,0:T(8,128)(2,1)S(1)}, u32[]{:S(2)}, u32[]{:S(2)}) %collective-permute-start.41) | collective-permute-done | bytes 1048608 | tf_op jit(solution)/shard_map/ppermute | solution.py:48
  884.6 15.1 %collective-permute-done.34 = bf16[2048,512]{1,0:T(8,128)(2,1)S(1)} collective-permute-done((bf16[2048,512]{1,0:T(8,128)(2,1)S(1)}, bf16[2048,512]{1,0:T(8,128)(2,1)S(1)}, u32[]{:S(2)}, u32[]{:S(2)}) %collective-permute-start.34) | collective-permute-done | bytes 2097184 | tf_op jit(solution)/shard_map/ppermute | solution.py:48
  911.1 33.7 %collective-permute-done.42 = bf16[2048,512]{1,0:T(8,128)(2,1)} collective-permute-done((bf16[2048,512]{1,0:T(8,128)(2,1)}, bf16[2048,512]{1,0:T(8,128)(2,1)}, u32[]{:S(2)}, u32[]{:S(2)}) %collective-permute-start.42) | collective-permute-done | bytes 2097184 | tf_op jit(solution)/shard_map/ppermute | solution.py:48
  954.9 30.2 %collective-permute-done.50 = bf16[1024,1024]{1,0:T(8,128)(2,1)S(1)} collective-permute-done((bf16[1024,1024]{1,0:T(8,128)(2,1)S(1)}, bf16[1024,1024]{1,0:T(8,128)(2,1)S(1)}, u32[]{:S(2)}, u32[]{:S(2)}) %collective-permute-start.50) | collective-permute-done | bytes 2097184 | tf_op jit(solution)/shard_map/ppermute | solution.py:48
  989.3 4.3 convert_select_fusion.5
  993.6 6.5 pad_maximum_fusion
  1000.2 4.0 convert_select_fusion.3
  1004.2 6.6 pad_maximum_fusion.1
  1014.9 6.5 pad_maximum_fusion.2
  (578 shorter events, 342.6 us)
Async XLA Ops:
  0.6 59.4 %collective-permute-start = (bf16[512]{0:T(512)(128)(2,1)}, bf16[512]{0:T(512)(128)(2,1)S(1)}, u32[]{:S(2)}, u32[]{:S(2)}) collective-permute-start(bf16[512]{0:T(512)(128)(2,1)} %param.20), channel_id=1, source_target_pairs={{0,1},{1,0},{2,3},{3,2},{4,5},{5,4},{6,7},{7,6},{8,9},{9,8},{10,11... | collective-permute-start | bytes 3080 | tf_op jit(solution)/shard_map/ppermute | solution.py:48
  8.9 16.4 %collective-permute-start.3 = (bf16[1,256,1152]{2,1,0:T(8,128)(2,1)S(1)}, bf16[1,256,1152]{2,1,0:T(8,128)(2,1)}, u32[]{:S(2)}, u32[]{:S(2)}) collective-permute-start(bf16[1,256,1152]{2,1,0:T(8,128)(2,1)S(1)} %dynamic-slice_bitcast_fusion.1), channel_id=1, source_target_pairs={{0,1},{1,0},{2,3},{3,2},{4,5},{5,4},{6,7},{7,6},{8,9},{9,8},{10,11... | collective-permute-start | bytes 1769480 | tf_op jit(solution)/shard_map/ppermute | solution.py:48
  11.0 36.8 %collective-permute-start.1 = (bf16[1,256,2048]{2,1,0:T(8,128)(2,1)}, bf16[1,256,2048]{2,1,0:T(8,128)(2,1)}, u32[]{:S(2)}, u32[]{:S(2)}) collective-permute-start(bf16[1,256,2048]{2,1,0:T(8,128)(2,1)} %fusion.80), channel_id=1, source_target_pairs={{0,1},{1,0},{2,3},{3,2},{4,5},{5,4},{6,7},{7,6},{8,9},{9,8},{10,11... | collective-permute-start | bytes 3145736 | tf_op jit(solution)/shard_map/ppermute | solution.py:48
  13.0 167.6 %collective-permute-start.8 = (bf16[512,1024]{1,0:T(8,128)(2,1)}, bf16[512,1024]{1,0:T(8,128)(2,1)}, u32[]{:S(2)}, u32[]{:S(2)}) collective-permute-start(bf16[512,1024]{1,0:T(8,128)(2,1)} %param.18), channel_id=1, source_target_pairs={{0,1},{1,0},{2,3},{3,2},{4,5},{5,4},{6,7},{7,6},{8,9},{9,8},{10,11... | collective-permute-start | bytes 3145736 | tf_op jit(solution)/shard_map/ppermute | solution.py:48
  27.7 32.4 %collective-permute-start.4 = (bf16[2,256,1152]{2,1,0:T(8,128)(2,1)}, bf16[2,256,1152]{2,1,0:T(8,128)(2,1)}, u32[]{:S(2)}, u32[]{:S(2)}) collective-permute-start(bf16[2,256,1152]{2,1,0:T(8,128)(2,1)} %pad_maximum_fusion.15), channel_id=1, source_target_pairs={{0,2},{2,0},{4,6},{6,4},{8,10},{10,8},{12,14},{14,12},{16,18},{18,... | collective-permute-start | bytes 3538952 | tf_op jit(solution)/shard_map/ppermute | solution.py:48
  51.0 12.6 %collective-permute-start.2 = (bf16[2,256,2048]{2,1,0:T(8,128)(2,1)}, bf16[2,256,2048]{2,1,0:T(8,128)(2,1)}, u32[]{:S(2)}, u32[]{:S(2)}) collective-permute-start(bf16[2,256,2048]{2,1,0:T(8,128)(2,1)} %pad_maximum_fusion.8), channel_id=1, source_target_pairs={{0,2},{2,0},{4,6},{6,4},{8,10},{10,8},{12,14},{14,12},{16,18},{18,... | collective-permute-start | bytes 6291464 | tf_op jit(solution)/shard_map/ppermute | solution.py:48
  154.5 28.9 %collective-permute-start.6 = (bf16[512,1024]{1,0:T(8,128)(2,1)}, bf16[512,1024]{1,0:T(8,128)(2,1)}, u32[]{:S(2)}, u32[]{:S(2)}) collective-permute-start(bf16[512,1024]{1,0:T(8,128)(2,1)} %multiply_convert_fusion.4), channel_id=1, source_target_pairs={{0,1},{1,0},{2,3},{3,2},{4,5},{5,4},{6,7},{7,6},{8,9},{9,8},{10,11... | collective-permute-start | bytes 3145736 | tf_op jit(solution)/shard_map/ppermute | solution.py:48
  154.5 26.1 %collective-permute-start.5 = (s32[512,8]{0,1:T(8,128)S(1)}, s32[512,8]{0,1:T(8,128)S(1)}, u32[]{:S(2)}, u32[]{:S(2)}) collective-permute-start(s32[512,8]{0,1:T(8,128)S(1)} %copy-done.61), channel_id=1, source_target_pairs={{0,1},{1,0},{2,3},{3,2},{4,5},{5,4},{6,7},{7,6},{8,9},{9,8},{10,11... | collective-permute-start | bytes 49160 | tf_op jit(solution)/shard_map/ppermute | solution.py:48
  328.7 41.5 %collective-permute-start.9 = (bf16[512,1024]{1,0:T(8,128)(2,1)}, bf16[512,1024]{1,0:T(8,128)(2,1)}, u32[]{:S(2)}, u32[]{:S(2)}) collective-permute-start(bf16[512,1024]{1,0:T(8,128)(2,1)} %constant_dynamic-slice_fusion.25), channel_id=1, source_target_pairs={{0,1},{1,0},{2,3},{3,2},{4,5},{5,4},{6,7},{7,6},{8,9},{9,8},{10,11... | collective-permute-start | bytes 3145736 | tf_op jit(solution)/shard_map/ppermute | solution.py:48
  330.0 46.3 %collective-permute-start.7 = (bf16[512,1024]{1,0:T(8,128)(2,1)}, bf16[512,1024]{1,0:T(8,128)(2,1)S(1)}, u32[]{:S(2)}, u32[]{:S(2)}) collective-permute-start(bf16[512,1024]{1,0:T(8,128)(2,1)} %constant_dynamic-slice_fusion.26), channel_id=1, source_target_pairs={{0,1},{1,0},{2,3},{3,2},{4,5},{5,4},{6,7},{7,6},{8,9},{9,8},{10,11... | collective-permute-start | bytes 3145736 | tf_op jit(solution)/shard_map/ppermute | solution.py:48
  349.0 203.5 %collective-permute-start.28 = (bf16[4096,512]{1,0:T(8,128)(2,1)}, bf16[4096,512]{1,0:T(8,128)(2,1)}, u32[]{:S(2)}, u32[]{:S(2)}) collective-permute-start(bf16[4096,512]{1,0:T(8,128)(2,1)} %constant_dynamic-slice_fusion.14), channel_id=1, source_target_pairs={{0,2},{2,0},{4,6},{6,4},{8,10},{10,8},{12,14},{14,12},{16,18},{18,... | collective-permute-start | bytes 12582920 | tf_op jit(solution)/shard_map/ppermute | solution.py:48
  364.9 207.1 %collective-permute-start.36 = (bf16[4096,512]{1,0:T(8,128)(2,1)}, bf16[4096,512]{1,0:T(8,128)(2,1)}, u32[]{:S(2)}, u32[]{:S(2)}) collective-permute-start(bf16[4096,512]{1,0:T(8,128)(2,1)} %constant_dynamic-slice_fusion.10), channel_id=1, source_target_pairs={{0,2},{2,0},{4,6},{6,4},{8,10},{10,8},{12,14},{14,12},{16,18},{18,... | collective-permute-start | bytes 12582920 | tf_op jit(solution)/shard_map/ppermute | solution.py:48
  370.1 250.9 %collective-permute-start.44 = (bf16[2048,1024]{1,0:T(8,128)(2,1)}, bf16[2048,1024]{1,0:T(8,128)(2,1)}, u32[]{:S(2)}, u32[]{:S(2)}) collective-permute-start(bf16[2048,1024]{1,0:T(8,128)(2,1)} %constant_dynamic-slice_fusion.6), channel_id=1, source_target_pairs={{0,2},{2,0},{4,6},{6,4},{8,10},{10,8},{12,14},{14,12},{16,18},{18,... | collective-permute-start | bytes 12582920 | tf_op jit(solution)/shard_map/ppermute | solution.py:48
  491.8 14.5 %collective-permute-start.20 = (bf16[1,256,1152]{2,1,0:T(8,128)(2,1)S(1)}, bf16[1,256,1152]{2,1,0:T(8,128)(2,1)}, u32[]{:S(2)}, u32[]{:S(2)}) collective-permute-start(bf16[1,256,1152]{2,1,0:T(8,128)(2,1)S(1)} %constant_dynamic-slice_fusion.18), channel_id=1, source_target_pairs={{0,1},{1,0},{2,3},{3,2},{4,5},{5,4},{6,7},{7,6},{8,9},{9,8},{10,11... | collective-permute-start | bytes 1769480 | tf_op jit(solution)/shard_map/ppermute | solution.py:48
  507.6 15.2 %collective-permute-start.21 = (bf16[1,128,1152]{2,1,0:T(8,128)(2,1)S(1)}, bf16[1,128,1152]{2,1,0:T(8,128)(2,1)S(1)}, u32[]{:S(2)}, u32[]{:S(2)}) collective-permute-start(bf16[1,128,1152]{2,1,0:T(8,128)(2,1)S(1)} %constant_dynamic-slice_fusion.17), channel_id=1, source_target_pairs={{0,4},{2,6},{4,0},{6,2},{8,12},{10,14},{12,8},{14,10},{16,20},{18,... | collective-permute-start | bytes 884744 | tf_op jit(solution)/shard_map/ppermute | solution.py:48
  526.4 15.1 %collective-permute-start.10 = (bf16[2,256,2176]{2,1,0:T(8,128)(2,1)S(1)}, bf16[2,256,2176]{2,1,0:T(8,128)(2,1)S(1)}, u32[]{:S(2)}, u32[]{:S(2)}) collective-permute-start(bf16[2,256,2176]{2,1,0:T(8,128)(2,1)S(1)} %constant_dynamic-slice_fusion.24), channel_id=1, source_target_pairs={{0,2},{2,0},{4,6},{6,4},{8,10},{10,8},{12,14},{14,12},{16,18},{18,... | collective-permute-start | bytes 6684680 | tf_op jit(solution)/shard_map/ppermute | solution.py:48
  539.0 5.7 collective-permute-start.25
  544.7 6.8 collective-permute-start.26
  546.4 22.4 %collective-permute-start.11 = (bf16[1,256,2176]{2,1,0:T(8,128)(2,1)}, bf16[1,256,2176]{2,1,0:T(8,128)(2,1)}, u32[]{:S(2)}, u32[]{:S(2)}) collective-permute-start(bf16[1,256,2176]{2,1,0:T(8,128)(2,1)} %constant_dynamic-slice_fusion.23), channel_id=1, source_target_pairs={{0,1},{1,0},{2,3},{3,2},{4,5},{5,4},{6,7},{7,6},{8,9},{9,8},{10,11... | collective-permute-start | bytes 3342344 | tf_op jit(solution)/shard_map/ppermute | solution.py:48
  552.5 83.4 %collective-permute-start.27 = (bf16[1,256,1152]{2,1,0:T(8,128)(2,1)}, bf16[1,256,1152]{2,1,0:T(8,128)(2,1)S(1)}, u32[]{:S(2)}, u32[]{:S(2)}) collective-permute-start(bf16[1,256,1152]{2,1,0:T(8,128)(2,1)} %pad_maximum_fusion.22), channel_id=1, source_target_pairs={{0,2},{2,0},{4,6},{6,4},{8,10},{10,8},{12,14},{14,12},{16,18},{18,... | collective-permute-start | bytes 1769480 | tf_op jit(solution)/shard_map/ppermute | solution.py:48
  558.1 87.1 %collective-permute-start.29 = (bf16[2048,512]{1,0:T(8,128)(2,1)}, bf16[2048,512]{1,0:T(8,128)(2,1)}, u32[]{:S(2)}, u32[]{:S(2)}) collective-permute-start(bf16[2048,512]{1,0:T(8,128)(2,1)} %constant_dynamic-slice_fusion.13), channel_id=1, source_target_pairs={{0,4},{2,6},{4,0},{6,2},{8,12},{10,14},{12,8},{14,10},{16,20},{18,... | collective-permute-start | bytes 6291464 | tf_op jit(solution)/shard_map/ppermute | solution.py:48
  570.4 48.4 %collective-permute-start.12 = (bf16[1,128,2176]{2,1,0:T(8,128)(2,1)S(1)}, bf16[1,128,2176]{2,1,0:T(8,128)(2,1)S(1)}, u32[]{:S(2)}, u32[]{:S(2)}) collective-permute-start(bf16[1,128,2176]{2,1,0:T(8,128)(2,1)S(1)} %constant_dynamic-slice_fusion.22), channel_id=1, source_target_pairs={{0,4},{2,6},{4,0},{6,2},{8,12},{10,14},{12,8},{14,10},{16,20},{18,... | collective-permute-start | bytes 1671176 | tf_op jit(solution)/shard_map/ppermute | solution.py:48
  575.7 88.1 %collective-permute-start.37 = (bf16[2048,512]{1,0:T(8,128)(2,1)S(1)}, bf16[2048,512]{1,0:T(8,128)(2,1)S(1)}, u32[]{:S(2)}, u32[]{:S(2)}) collective-permute-start(bf16[2048,512]{1,0:T(8,128)(2,1)S(1)} %constant_dynamic-slice_fusion.9), channel_id=1, source_target_pairs={{0,4},{2,6},{4,0},{6,2},{8,12},{10,14},{12,8},{14,10},{16,20},{18,... | collective-permute-start | bytes 6291464 | tf_op jit(solution)/shard_map/ppermute | solution.py:48
  619.0 7.7 collective-permute-start.13
  626.8 7.6 collective-permute-start.14
  630.0 77.6 %collective-permute-start.45 = (bf16[1024,1024]{1,0:T(8,128)(2,1)S(1)}, bf16[1024,1024]{1,0:T(8,128)(2,1)S(1)}, u32[]{:S(2)}, u32[]{:S(2)}) collective-permute-start(bf16[1024,1024]{1,0:T(8,128)(2,1)S(1)} %constant_dynamic-slice_fusion.5), channel_id=1, source_target_pairs={{0,4},{2,6},{4,0},{6,2},{8,12},{10,14},{12,8},{14,10},{16,20},{18,... | collective-permute-start | bytes 6291464 | tf_op jit(solution)/shard_map/ppermute | solution.py:48
  634.4 6.1 collective-permute-start.15
  640.5 73.9 %collective-permute-start.16 = (bf16[1,64,2176]{2,1,0:T(8,128)(2,1)S(1)}, bf16[1,64,2176]{2,1,0:T(8,128)(2,1)S(1)}, u32[]{:S(2)}, u32[]{:S(2)}) collective-permute-start(bf16[1,64,2176]{2,1,0:T(8,128)(2,1)S(1)} %pad_maximum_fusion.25), channel_id=1, source_target_pairs={{0,8},{2,10},{4,12},{6,14},{8,0},{10,2},{12,4},{14,6},{16,24},{18,... | collective-permute-start | bytes 835592 | tf_op jit(solution)/shard_map/ppermute | solution.py:48
  647.5 63.5 %collective-permute-start.30 = (bf16[1024,512]{1,0:T(8,128)(2,1)S(1)}, bf16[1024,512]{1,0:T(8,128)(2,1)S(1)}, u32[]{:S(2)}, u32[]{:S(2)}) collective-permute-start(bf16[1024,512]{1,0:T(8,128)(2,1)S(1)} %constant_dynamic-slice_fusion.12), channel_id=1, source_target_pairs={{0,8},{2,10},{4,12},{6,14},{8,0},{10,2},{12,4},{14,6},{16,24},{18,... | collective-permute-start | bytes 3145736 | tf_op jit(solution)/shard_map/ppermute | solution.py:48
  664.5 50.0 %collective-permute-start.38 = (bf16[1024,512]{1,0:T(8,128)(2,1)S(1)}, bf16[1024,512]{1,0:T(8,128)(2,1)S(1)}, u32[]{:S(2)}, u32[]{:S(2)}) collective-permute-start(bf16[1024,512]{1,0:T(8,128)(2,1)S(1)} %constant_dynamic-slice_fusion.8), channel_id=1, source_target_pairs={{0,8},{2,10},{4,12},{6,14},{8,0},{10,2},{12,4},{14,6},{16,24},{18,... | collective-permute-start | bytes 3145736 | tf_op jit(solution)/shard_map/ppermute | solution.py:48
  708.9 38.6 %collective-permute-start.46 = (bf16[512,1024]{1,0:T(8,128)(2,1)S(1)}, bf16[512,1024]{1,0:T(8,128)(2,1)S(1)}, u32[]{:S(2)}, u32[]{:S(2)}) collective-permute-start(bf16[512,1024]{1,0:T(8,128)(2,1)S(1)} %constant_dynamic-slice_fusion.4), channel_id=1, source_target_pairs={{0,8},{2,10},{4,12},{6,14},{8,0},{10,2},{12,4},{14,6},{16,24},{18,... | collective-permute-start | bytes 3145736 | tf_op jit(solution)/shard_map/ppermute | solution.py:48
  711.4 32.5 %collective-permute-start.31 = (bf16[512,512]{1,0:T(8,128)(2,1)S(1)}, bf16[512,512]{1,0:T(8,128)(2,1)S(1)}, u32[]{:S(2)}, u32[]{:S(2)}) collective-permute-start(bf16[512,512]{1,0:T(8,128)(2,1)S(1)} %constant_dynamic-slice_fusion.11), channel_id=1, source_target_pairs={{0,16},{2,18},{4,20},{6,22},{8,24},{10,26},{12,28},{14,30},{16,0},... | collective-permute-start | bytes 1572872 | tf_op jit(solution)/shard_map/ppermute | solution.py:48
  744.0 50.1 %collective-permute-start.32 = (bf16[512,512]{1,0:T(8,128)(2,1)S(1)}, bf16[512,512]{1,0:T(8,128)(2,1)S(1)}, u32[]{:S(2)}, u32[]{:S(2)}) collective-permute-start(bf16[512,512]{1,0:T(8,128)(2,1)S(1)} %add_convert_fusion.20), channel_id=1, source_target_pairs={{0,16},{2,18},{4,20},{6,22},{8,24},{10,26},{12,28},{14,30},{16,0},... | collective-permute-start | bytes 1572872 | tf_op jit(solution)/shard_map/ppermute | solution.py:48
  747.5 57.8 %collective-permute-start.39 = (bf16[512,512]{1,0:T(8,128)(2,1)S(1)}, bf16[512,512]{1,0:T(8,128)(2,1)S(1)}, u32[]{:S(2)}, u32[]{:S(2)}) collective-permute-start(bf16[512,512]{1,0:T(8,128)(2,1)S(1)} %constant_dynamic-slice_fusion.7), channel_id=1, source_target_pairs={{0,16},{2,18},{4,20},{6,22},{8,24},{10,26},{12,28},{14,30},{16,0},... | collective-permute-start | bytes 1572872 | tf_op jit(solution)/shard_map/ppermute | solution.py:48
  748.0 69.8 %collective-permute-start.47 = (bf16[256,1024]{1,0:T(8,128)(2,1)S(1)}, bf16[256,1024]{1,0:T(8,128)(2,1)S(1)}, u32[]{:S(2)}, u32[]{:S(2)}) collective-permute-start(bf16[256,1024]{1,0:T(8,128)(2,1)S(1)} %constant_dynamic-slice_fusion.3), channel_id=1, source_target_pairs={{0,16},{2,18},{4,20},{6,22},{8,24},{10,26},{12,28},{14,30},{16,0},... | collective-permute-start | bytes 1572872 | tf_op jit(solution)/shard_map/ppermute | solution.py:48
  794.3 56.2 %collective-permute-start.33 = (bf16[1024,512]{1,0:T(8,128)(2,1)S(1)}, bf16[1024,512]{1,0:T(8,128)(2,1)S(1)}, u32[]{:S(2)}, u32[]{:S(2)}) collective-permute-start(bf16[1024,512]{1,0:T(8,128)(2,1)S(1)} %pad_maximum_fusion.17), channel_id=1, source_target_pairs={{0,8},{2,10},{4,12},{6,14},{8,0},{10,2},{12,4},{14,6},{16,24},{18,... | collective-permute-start | bytes 3145736 | tf_op jit(solution)/shard_map/ppermute | solution.py:48
  805.5 44.8 %collective-permute-start.40 = (bf16[512,512]{1,0:T(8,128)(2,1)S(1)}, bf16[512,512]{1,0:T(8,128)(2,1)S(1)}, u32[]{:S(2)}, u32[]{:S(2)}) collective-permute-start(bf16[512,512]{1,0:T(8,128)(2,1)S(1)} %add_convert_fusion.19), channel_id=1, source_target_pairs={{0,16},{2,18},{4,20},{6,22},{8,24},{10,26},{12,28},{14,30},{16,0},... | collective-permute-start | bytes 1572872 | tf_op jit(solution)/shard_map/ppermute | solution.py:48
  805.6 46.1 %collective-permute-start.17 = (bf16[1,128,2176]{2,1,0:T(8,128)(2,1)S(1)}, bf16[1,128,2176]{2,1,0:T(8,128)(2,1)S(1)}, u32[]{:S(2)}, u32[]{:S(2)}) collective-permute-start(bf16[1,128,2176]{2,1,0:T(8,128)(2,1)S(1)} %pad_maximum_fusion.23), channel_id=1, source_target_pairs={{0,4},{2,6},{4,0},{6,2},{8,12},{10,14},{12,8},{14,10},{16,20},{18,... | collective-permute-start | bytes 1671176 | tf_op jit(solution)/shard_map/ppermute | solution.py:48
  818.0 41.5 %collective-permute-start.48 = (bf16[256,1024]{1,0:T(8,128)(2,1)S(1)}, bf16[256,1024]{1,0:T(8,128)(2,1)S(1)}, u32[]{:S(2)}, u32[]{:S(2)}) collective-permute-start(bf16[256,1024]{1,0:T(8,128)(2,1)S(1)} %add_convert_fusion.18), channel_id=1, source_target_pairs={{0,16},{2,18},{4,20},{6,22},{8,24},{10,26},{12,28},{14,30},{16,0},... | collective-permute-start | bytes 1572872 | tf_op jit(solution)/shard_map/ppermute | solution.py:48
  850.5 31.5 %collective-permute-start.41 = (bf16[1024,512]{1,0:T(8,128)(2,1)S(1)}, bf16[1024,512]{1,0:T(8,128)(2,1)S(1)}, u32[]{:S(2)}, u32[]{:S(2)}) collective-permute-start(bf16[1024,512]{1,0:T(8,128)(2,1)S(1)} %pad_maximum_fusion.18), channel_id=1, source_target_pairs={{0,8},{2,10},{4,12},{6,14},{8,0},{10,2},{12,4},{14,6},{16,24},{18,... | collective-permute-start | bytes 3145736 | tf_op jit(solution)/shard_map/ppermute | solution.py:48
  851.1 48.6 %collective-permute-start.34 = (bf16[2048,512]{1,0:T(8,128)(2,1)S(1)}, bf16[2048,512]{1,0:T(8,128)(2,1)S(1)}, u32[]{:S(2)}, u32[]{:S(2)}) collective-permute-start(bf16[2048,512]{1,0:T(8,128)(2,1)S(1)} %pad_maximum_fusion.12), channel_id=1, source_target_pairs={{0,4},{2,6},{4,0},{6,2},{8,12},{10,14},{12,8},{14,10},{16,20},{18,... | collective-permute-start | bytes 6291464 | tf_op jit(solution)/shard_map/ppermute | solution.py:48
  853.1 56.0 %collective-permute-start.18 = (bf16[1,256,2176]{2,1,0:T(8,128)(2,1)}, bf16[1,256,2176]{2,1,0:T(8,128)(2,1)}, u32[]{:S(2)}, u32[]{:S(2)}) collective-permute-start(bf16[1,256,2176]{2,1,0:T(8,128)(2,1)} %pad_maximum_fusion.16), channel_id=1, source_target_pairs={{0,2},{2,0},{4,6},{6,4},{8,10},{10,8},{12,14},{14,12},{16,18},{18,... | collective-permute-start | bytes 3342344 | tf_op jit(solution)/shard_map/ppermute | solution.py:48
  860.8 45.4 %collective-permute-start.49 = (bf16[512,1024]{1,0:T(8,128)(2,1)}, bf16[512,1024]{1,0:T(8,128)(2,1)}, u32[]{:S(2)}, u32[]{:S(2)}) collective-permute-start(bf16[512,1024]{1,0:T(8,128)(2,1)} %pad_maximum_fusion.19), channel_id=1, source_target_pairs={{0,8},{2,10},{4,12},{6,14},{8,0},{10,2},{12,4},{14,6},{16,24},{18,... | collective-permute-start | bytes 3145736 | tf_op jit(solution)/shard_map/ppermute | solution.py:48
  884.1 60.7 %collective-permute-start.42 = (bf16[2048,512]{1,0:T(8,128)(2,1)}, bf16[2048,512]{1,0:T(8,128)(2,1)}, u32[]{:S(2)}, u32[]{:S(2)}) collective-permute-start(bf16[2048,512]{1,0:T(8,128)(2,1)} %pad_maximum_fusion.13), channel_id=1, source_target_pairs={{0,4},{2,6},{4,0},{6,2},{8,12},{10,14},{12,8},{14,10},{16,20},{18,... | collective-permute-start | bytes 6291464 | tf_op jit(solution)/shard_map/ppermute | solution.py:48
  903.2 85.9 %collective-permute-start.35 = (bf16[4096,512]{1,0:T(8,128)(2,1)}, bf16[4096,512]{1,0:T(8,128)(2,1)}, u32[]{:S(2)}, u32[]{:S(2)}) collective-permute-start(bf16[4096,512]{1,0:T(8,128)(2,1)} %pad_maximum_fusion.4), channel_id=1, source_target_pairs={{0,2},{2,0},{4,6},{6,4},{8,10},{10,8},{12,14},{14,12},{16,18},{18,... | collective-permute-start | bytes 12582920 | tf_op jit(solution)/shard_map/ppermute | solution.py:48
  908.5 76.6 %collective-permute-start.50 = (bf16[1024,1024]{1,0:T(8,128)(2,1)S(1)}, bf16[1024,1024]{1,0:T(8,128)(2,1)S(1)}, u32[]{:S(2)}, u32[]{:S(2)}) collective-permute-start(bf16[1024,1024]{1,0:T(8,128)(2,1)S(1)} %pad_maximum_fusion.14), channel_id=1, source_target_pairs={{0,4},{2,6},{4,0},{6,2},{8,12},{10,14},{12,8},{14,10},{16,20},{18,... | collective-permute-start | bytes 6291464 | tf_op jit(solution)/shard_map/ppermute | solution.py:48
  949.5 50.7 %collective-permute-start.43 = (bf16[4096,512]{1,0:T(8,128)(2,1)}, bf16[4096,512]{1,0:T(8,128)(2,1)}, u32[]{:S(2)}, u32[]{:S(2)}) collective-permute-start(bf16[4096,512]{1,0:T(8,128)(2,1)} %pad_maximum_fusion.5), channel_id=1, source_target_pairs={{0,2},{2,0},{4,6},{6,4},{8,10},{10,8},{12,14},{14,12},{16,18},{18,... | collective-permute-start | bytes 12582920 | tf_op jit(solution)/shard_map/ppermute | solution.py:48
  989.0 21.8 %collective-permute-start.51 = (bf16[2048,1024]{1,0:T(8,128)(2,1)}, bf16[2048,1024]{1,0:T(8,128)(2,1)}, u32[]{:S(2)}, u32[]{:S(2)}) collective-permute-start(bf16[2048,1024]{1,0:T(8,128)(2,1)} %pad_maximum_fusion.6), channel_id=1, source_target_pairs={{0,2},{2,0},{4,6},{6,4},{8,10},{10,8},{12,14},{14,12},{16,18},{18,... | collective-permute-start | bytes 12582920 | tf_op jit(solution)/shard_map/ppermute | solution.py:48
  (80 other events, 1042.3 us)

commit v2 on v1

v2 whole, which is shorter than its diff:
```python
import functools

import jax
import jax.numpy as jnp
from jax import lax
from jax.experimental import pallas as pl
from jax.experimental.pallas import tpu as pltpu
from jax.sharding import PartitionSpec as P

HQ = 16
KV = 8
HD = 64
E = 16
GRP = 2


norm_eps = 1e-06
residual_scale = 0.22
score_scale = 0.015625
rope_base = 10000.0
masked_value = -1e30


def rope_tables(length):
    positions = jnp.arange(length, dtype=jnp.float32)
    inverse = rope_base ** (-jnp.arange(0, HD, 2, dtype=jnp.float32) / HD)
    angles = positions[:, None] * inverse[None, :]
    cosine_table = jnp.cos(angles)
    sine_table = jnp.sin(angles)
    return (
        jnp.concatenate([cosine_table, cosine_table], -1),
        jnp.concatenate([sine_table, sine_table], -1),
    )


def swap(values, axis, size, bit):
    return lax.ppermute(values, axis, [(i, i ^ bit) for i in range(size)])


def side_of(axis, bit):
    return (lax.axis_index(axis) // bit) % 2


def bits_of(size):
    return [1 << place for place in range(size.bit_length() - 1)]


def fold(values, dim, axis, size, bit):
    side = side_of(axis, bit)
    half = values.shape[dim] // 2
    send = lax.dynamic_slice_in_dim(values, (1 - side) * half, half, dim)
    keep = lax.dynamic_slice_in_dim(values, side * half, half, dim)
    received = swap(send, axis, size, bit)
    return (keep.astype(jnp.float32) + received.astype(jnp.float32)).astype(jnp.bfloat16)


def unfold(values, dim, axis, size, bit, kept=jnp.bfloat16):
    side = side_of(axis, bit)
    other = swap(values, axis, size, bit).astype(kept)
    values = values.astype(kept)
    lower = jnp.where(side == 0, values, other)
    upper = jnp.where(side == 0, other, values)
    return jnp.concatenate([lower, upper], dim)


def group_gather(values, groups):
    for bit in bits_of(groups):
        values = unfold(values, 0, "group", groups, bit, values.dtype)
    return values


def group_scatter(values, groups):
    for bit in reversed(bits_of(groups)):
        values = fold(values, 0, "group", groups, bit)
    return values


def gather_rows(values, replicas, groups):
    rows, columns = values.shape
    half = rows // 2
    part = lax.dynamic_slice_in_dim(values, side_of("replica", 1) * half, half, 0)
    part = group_gather(part[None], groups)
    return unfold(part, 1, "replica", replicas, 1).reshape(groups * rows, columns)


def join_kernel(side_ref, own_ref, other_ref, out_ref):
    own_here = pl.program_id(0) // (pl.num_programs(0) // 2) == side_ref[0]

    @pl.when(own_here)
    def _():
        out_ref[...] = own_ref[...].astype(jnp.float32)

    @pl.when(jnp.logical_not(own_here))
    def _():
        out_ref[...] = other_ref[...].astype(jnp.float32)


def join_halves(values, replicas):
    rows, columns = values.shape
    other = swap(values, "replica", replicas, 1)
    parts = 4
    half_spec = pl.BlockSpec((rows // parts, columns), lambda i, side: (i % parts, 0))
    return pl.pallas_call(
        join_kernel,
        grid_spec=pltpu.PrefetchScalarGridSpec(
            num_scalar_prefetch=1,
            grid=(2 * parts,),
            in_specs=[half_spec, half_spec],
            out_specs=pl.BlockSpec((rows // parts, columns), lambda i, side: (i, 0)),
        ),
        out_shape=jax.ShapeDtypeStruct((2 * rows, columns), jnp.float32),
        compiler_params=pltpu.CompilerParams(vmem_limit_bytes=24 * 1024 * 1024),
        cost_estimate=pl.CostEstimate(
            flops=0, bytes_accessed=16 * rows * columns, transcendentals=0
        ),
    )(side_of("replica", 1).astype(jnp.int32).reshape(1), values, other)


def sum_step(values, replicas, place, swapped=False):
    bits = bits_of(replicas)
    if swapped:
        bits = bits[:1] + bits[2:] + bits[1:2]
    if place < len(bits):
        return fold(values, 0, "replica", replicas, bits[place])
    if place == 2 * len(bits) - 1:
        return join_halves(values, replicas)
    return unfold(values, 0, "replica", replicas, bits[2 * len(bits) - 1 - place])


def flat_rows(values):
    return values.astype(jnp.bfloat16).reshape(-1, values.shape[-1])


def small_step(values, replicas, groups, place):
    bits = bits_of(replicas)
    if place == 1:
        return group_scatter(values, groups)
    place = place if place == 0 else place - 1
    if place < len(bits):
        return fold(values, 1, "replica", replicas, bits[place])
    return unfold(values, 1, "replica", replicas, bits[2 * len(bits) - 1 - place])


def lane_side(width):
    return lax.broadcasted_iota(jnp.int32, (1, width), 1) // HD % 2


def turned_lanes(block):
    first = lax.broadcasted_iota(jnp.int32, (1, 2 * HD), 1) % HD < HD // 2
    return jnp.where(first, -pltpu.roll(block, 3 * HD // 2, 1), pltpu.roll(block, HD // 2, 1))


def turned_back(block):
    first = lax.broadcasted_iota(jnp.int32, (1, 2 * HD), 1) % HD < HD // 2
    return jnp.where(first, pltpu.roll(block, 3 * HD // 2, 1), -pltpu.roll(block, HD // 2, 1))


def both_sides(block, head):
    own = jnp.where(lane_side(2 * HD) == head, block, 0.0)
    moved = pltpu.roll(own, HD, 1)
    pair = (own, moved) if head == 0 else (moved, own)
    return [part.astype(jnp.bfloat16) for part in pair]


def lanes_dot(left, right):
    return lax.dot_general(
        left, right, (((1,), (1,)), ((), ())), preferred_element_type=jnp.float32
    )


def rows_dot(left, right):
    return lax.dot_general(
        left, right, (((0,), (0,)), ((), ())), preferred_element_type=jnp.float32
    )


def forward_kernel(query_ref, key_ref, value_ref, cos_ref, sin_ref, mix_ref):
    cosine, sine = cos_ref[...], sin_ref[...]
    length = query_ref.shape[0]
    step = min(256, length)
    key_raw = key_ref[...]
    key_block = (key_raw * cosine + turned_lanes(key_raw) * sine).astype(jnp.bfloat16)
    key_block = key_block.astype(jnp.float32) * score_scale
    value_block = value_ref[...]
    for head in range(2):
        lanes = slice(2 * HD * head, 2 * HD * (head + 1))
        query_raw = query_ref[:, lanes]
        query_pair = (query_raw * cosine + turned_lanes(query_raw) * sine).astype(jnp.bfloat16)
        key_sides = both_sides(key_block, head)
        value_sides = both_sides(value_block, head)
        for start in range(0, length, step):
            end = start + step
            row = lax.broadcasted_iota(jnp.int32, (step, end), 0) + start
            column = lax.broadcasted_iota(jnp.int32, (step, end), 1)
            total = None
            for key_side, value_side in zip(key_sides, value_sides):
                scores = lanes_dot(query_pair[start:end], key_side[:end])
                scores = jnp.where(row >= column, scores, masked_value)
                exponent = jnp.exp(scores - jnp.max(scores, axis=1, keepdims=True))
                inverse = 1.0 / jnp.sum(exponent, axis=1, keepdims=True)
                rounded = (exponent * inverse).astype(jnp.bfloat16)
                part = jnp.dot(rounded, value_side[:end], preferred_element_type=jnp.float32)
                total = part if total is None else total + part
            mix_ref[start:end, lanes] = total.astype(jnp.bfloat16)


def backward_kernel(
    query_ref, key_ref, value_ref, grad_ref, cos_ref, sin_ref, dquery_ref, dkey_ref, dvalue_ref
):
    cosine, sine = cos_ref[...], sin_ref[...]
    length = query_ref.shape[0]
    step = min(256, length)
    key_raw = key_ref[...]
    key_block = (key_raw * cosine + turned_lanes(key_raw) * sine).astype(jnp.bfloat16)
    key_block = key_block.astype(jnp.float32) * score_scale
    value_block = value_ref[...]
    side_lane = lane_side(2 * HD)
    key_total, value_total = None, None
    for head in range(2):
        lanes = slice(2 * HD * head, 2 * HD * (head + 1))
        query_raw = query_ref[:, lanes]
        query_pair = (query_raw * cosine + turned_lanes(query_raw) * sine).astype(jnp.bfloat16)
        grad_pair = grad_ref[:, lanes]
        key_sides = both_sides(key_block, head)
        value_sides = both_sides(value_block, head)
        query_grads = [0.0 for _ in range(0, length, step)]
        for side in range(2):
            key_side, value_side = key_sides[side], value_sides[side]
            key_grads = [0.0 for _ in range(0, length, step)]
            value_grads = [0.0 for _ in range(0, length, step)]
            for place in range(length // step):
                start = place * step
                end = start + step
                column = lax.broadcasted_iota(jnp.int32, (end, step), 0)
                row = lax.broadcasted_iota(jnp.int32, (end, step), 1) + start
                scores = lanes_dot(key_side[:end], query_pair[start:end])
                scores = jnp.where(row >= column, scores, masked_value)
                exponent = jnp.exp(scores - jnp.max(scores, axis=0, keepdims=True))
                probability = exponent * (1.0 / jnp.sum(exponent, axis=0, keepdims=True))
                grad_prob = lanes_dot(value_side[:end], grad_pair[start:end])
                inner = jnp.sum(probability * grad_prob, axis=0, keepdims=True)
                grad_scores = (probability * (grad_prob - inner)).astype(jnp.bfloat16)
                rounded = probability.astype(jnp.bfloat16)
                query_grads[place] += rows_dot(grad_scores, key_side[:end])
                key_part = jnp.dot(
                    grad_scores, query_pair[start:end], preferred_element_type=jnp.float32
                )
                value_part = jnp.dot(
                    rounded, grad_pair[start:end], preferred_element_type=jnp.float32
                )
                for other in range(place + 1):
                    rows = slice(other * step, (other + 1) * step)
                    key_grads[other] += key_part[rows]
                    value_grads[other] += value_part[rows]
            key_own = jnp.where(side_lane == side, jnp.concatenate(key_grads, 0), 0.0)
            value_own = jnp.where(side_lane == side, jnp.concatenate(value_grads, 0), 0.0)
            if side != head:
                key_own = pltpu.roll(key_own, HD, 1)
                value_own = pltpu.roll(value_own, HD, 1)
            key_total = key_own if key_total is None else key_total + key_own
            value_total = value_own if value_total is None else value_total + value_own
        query_grad = jnp.concatenate(query_grads, 0)
        dquery_ref[:, lanes] = (query_grad * cosine + turned_back(query_grad * sine)).astype(
            jnp.bfloat16
        )
    key_total = key_total * score_scale
    dkey_ref[...] = (key_total * cosine + turned_back(key_total * sine)).astype(jnp.bfloat16)
    dvalue_ref[...] = value_total.astype(jnp.bfloat16)


def attention_specs(length):
    pair = 2 * HD
    first_key = HQ * HD // pair
    first_value = first_key + KV * HD // pair
    query_spec = pl.BlockSpec((length, GRP * pair), lambda i: (0, i))
    key_spec = pl.BlockSpec((length, pair), lambda i: (0, first_key + i))
    value_spec = pl.BlockSpec((length, pair), lambda i: (0, first_value + i))
    table_spec = pl.BlockSpec((length, pair), lambda i: (0, 0))
    narrow_spec = pl.BlockSpec((length, pair), lambda i: (0, i))
    return query_spec, key_spec, value_spec, table_spec, narrow_spec


def attend_forward(projected, cosine, sine):
    length = projected.shape[0]
    query_spec, key_spec, value_spec, table_spec, _ = attention_specs(length)
    return pl.pallas_call(
        forward_kernel,
        grid=(KV // 2,),
        in_specs=[query_spec, key_spec, value_spec, table_spec, table_spec],
        out_specs=query_spec,
        out_shape=jax.ShapeDtypeStruct((length, HQ * HD), jnp.bfloat16),
        compiler_params=pltpu.CompilerParams(vmem_limit_bytes=32 * 1024 * 1024),
        cost_estimate=pl.CostEstimate(
            flops=4 * HQ * HD * length * length,
            bytes_accessed=12 * length * HQ * HD,
            transcendentals=HQ * length * length,
        ),
    )(projected, projected, projected, cosine, sine)


def attend_backward(projected, grad_mix, cosine, sine):
    length = projected.shape[0]
    query_spec, key_spec, value_spec, table_spec, narrow_spec = attention_specs(length)
    return pl.pallas_call(
        backward_kernel,
        grid=(KV // 2,),
        in_specs=[query_spec, key_spec, value_spec, query_spec, table_spec, table_spec],
        out_specs=[query_spec, narrow_spec, narrow_spec],
        out_shape=[
            jax.ShapeDtypeStruct((length, HQ * HD), jnp.bfloat16),
            jax.ShapeDtypeStruct((length, KV * HD), jnp.bfloat16),
            jax.ShapeDtypeStruct((length, KV * HD), jnp.bfloat16),
        ],
        compiler_params=pltpu.CompilerParams(vmem_limit_bytes=32 * 1024 * 1024),
        cost_estimate=pl.CostEstimate(
            flops=10 * HQ * HD * length * length,
            bytes_accessed=16 * length * HQ * HD,
            transcendentals=HQ * length * length,
        ),
    )(projected, projected, projected, grad_mix, cosine, sine)


def expert_kernel(
    rows_ref,
    turned_ref,
    cotangent_ref,
    gates_ref,
    gate_ref,
    up_ref,
    down_ref,
    moe_ref,
    grad_rows_ref,
    grad_gates_ref,
    gate_grad_ref,
    up_grad_ref,
    down_grad_ref,
    hidden_scratch,
    gate_scratch,
    up_scratch,
):
    expert = pl.program_id(0)
    own_lane = lax.broadcasted_iota(jnp.int32, (1, 128), 1) == expert
    step = 256

    @pl.when(expert == 0)
    def _():
        moe_ref[...] = jnp.zeros_like(moe_ref)
        grad_rows_ref[...] = jnp.zeros_like(grad_rows_ref)
        grad_gates_ref[...] = jnp.zeros_like(grad_gates_ref)

    def row_tile(place, carry):
        rows = pl.ds(pl.multiple_of(place * step, step), step)
        block = rows_ref[rows, :]
        gate_pre = jnp.dot(block, gate_ref[0], preferred_element_type=jnp.float32)
        up_pre = jnp.dot(block, up_ref[0], preferred_element_type=jnp.float32)
        grad_plain = residual_scale * lanes_dot(cotangent_ref[rows, :], down_ref[0])
        gates = jnp.sum(jnp.where(own_lane, gates_ref[rows, :], 0.0), axis=1, keepdims=True)
        sigmoid_gate = 1.0 / (1.0 + jnp.exp(-gate_pre))
        swish_gate = gate_pre * sigmoid_gate
        hidden = swish_gate * up_pre
        hidden_gated = (gates * hidden).astype(jnp.bfloat16)
        inner = jnp.sum(grad_plain * hidden, axis=1, keepdims=True)
        grad_gates_ref[rows, :] += jnp.where(own_lane, inner, 0.0)
        grad_hidden = gates * grad_plain
        grad_gate = (
            grad_hidden * up_pre * sigmoid_gate * (1.0 + gate_pre * (1.0 - sigmoid_gate))
        ).astype(jnp.bfloat16)
        grad_up = (grad_hidden * swish_gate).astype(jnp.bfloat16)
        hidden_scratch[rows, :] = hidden_gated
        gate_scratch[rows, :] = grad_gate
        up_scratch[rows, :] = grad_up
        moe_ref[rows, :] += jnp.dot(hidden_gated, down_ref[0], preferred_element_type=jnp.float32)
        grad_rows_ref[rows, :] += lanes_dot(grad_gate, gate_ref[0]) + lanes_dot(
            grad_up, up_ref[0]
        )
        return carry

    lax.fori_loop(0, rows_ref.shape[0] // step, row_tile, 0)

    def width_tile(place, carry):
        rows = pl.ds(pl.multiple_of(place * step, step), step)
        block = turned_ref[rows, :]
        gate_grad_ref[0, rows, :] = jnp.dot(
            block, gate_scratch[...], preferred_element_type=jnp.float32
        ).astype(jnp.bfloat16)
        up_grad_ref[0, rows, :] = jnp.dot(
            block, up_scratch[...], preferred_element_type=jnp.float32
        ).astype(jnp.bfloat16)
        return carry

    lax.fori_loop(0, turned_ref.shape[0] // step, width_tile, 0)
    for start in range(0, hidden_scratch.shape[1], step):
        part = rows_dot(hidden_scratch[:, start : start + step], cotangent_ref[...])
        down_grad_ref[0, start : start + step, :] = (residual_scale * part).astype(jnp.bfloat16)


def run_experts(rows, cotangent, gates, gate_weight, up_weight, down_weight):
    length, width = rows.shape
    experts, _, inner = gate_weight.shape
    whole_spec = lambda shape: pl.BlockSpec(
        shape, lambda e: (0, 0), pipeline_mode=pl.Buffered(1)
    )
    total_spec = lambda columns: pl.BlockSpec((length, columns), lambda e: (0, 0))
    wide_spec = pl.BlockSpec((1, width, inner), lambda e: (e, 0, 0))
    tall_spec = pl.BlockSpec((1, inner, width), lambda e: (e, 0, 0))
    padded = jnp.concatenate([gates, jnp.zeros((length, 128 - experts), jnp.float32)], 1)
    return pl.pallas_call(
        expert_kernel,
        grid=(experts,),
        in_specs=[
            whole_spec((length, width)),
            whole_spec((width, length)),
            whole_spec((length, width)),
            whole_spec((length, 128)),
            wide_spec,
            wide_spec,
            tall_spec,
        ],
        out_specs=[
            total_spec(width),
            total_spec(width),
            total_spec(128),
            wide_spec,
            wide_spec,
            tall_spec,
        ],
        out_shape=[
            jax.ShapeDtypeStruct((length, width), jnp.float32),
            jax.ShapeDtypeStruct((length, width), jnp.float32),
            jax.ShapeDtypeStruct((length, 128), jnp.float32),
            jax.ShapeDtypeStruct(gate_weight.shape, jnp.bfloat16),
            jax.ShapeDtypeStruct(up_weight.shape, jnp.bfloat16),
            jax.ShapeDtypeStruct(down_weight.shape, jnp.bfloat16),
        ],
        scratch_shapes=[pltpu.VMEM((length, inner), jnp.bfloat16) for _ in range(3)],
        compiler_params=pltpu.CompilerParams(vmem_limit_bytes=56 * 1024 * 1024),
        cost_estimate=pl.CostEstimate(
            flops=18 * experts * length * width * inner,
            bytes_accessed=12 * experts * width * inner,
            transcendentals=experts * length * inner,
        ),
    )(rows, rows.T, cotangent, padded, gate_weight, up_weight, down_weight)


def shards(
    replicas,
    groups,
    tokens,
    cotangent,
    routes,
    first_gain,
    query_weight,
    key_weight,
    value_weight,
    output_weight,
    second_gain,
    router_weight,
    gate_weight,
    up_weight,
    down_weight,
):
    length = tokens.shape[0]
    local_experts = gate_weight.shape[0]
    query_width = query_weight.shape[1]
    key_width = key_weight.shape[1]
    spare = 128 - E - 2
    wide = jnp.concatenate([query_weight, key_weight, value_weight], 1)
    late = jnp.concatenate(
        [
            output_weight,
            router_weight,
            second_gain[:, None],
            first_gain[:, None],
            jnp.zeros((output_weight.shape[0], spare), jnp.bfloat16),
        ],
        1,
    )
    gain_one = group_gather(first_gain, groups)
    wide_full = gather_rows(wide, replicas, groups)
    late_full = gather_rows(late, replicas, groups)
    routes_all = group_gather(routes, groups)
    cotangent_all = group_gather(cotangent, groups)
    output_width = output_weight.shape[1]
    output_full = late_full[:, :output_width]
    router_full = late_full[:, output_width : output_width + E]
    gain_two = late_full[:, output_width + E]
    tokens_float = tokens.astype(jnp.float32)
    scale_one = lax.rsqrt(jnp.mean(tokens_float * tokens_float, axis=-1, keepdims=True) + norm_eps)
    normed_one = (tokens_float * scale_one * gain_one.astype(jnp.float32)).astype(jnp.bfloat16)
    cosine_table, sine_table = rope_tables(length)
    cosine_pair = jnp.concatenate([cosine_table, cosine_table], 1)
    sine_pair = jnp.concatenate([sine_table, sine_table], 1)
    projected = jnp.dot(normed_one, wide_full, preferred_element_type=jnp.float32)
    attention_mix = attend_forward(projected, cosine_pair, sine_pair)
    attention_out = jnp.dot(attention_mix, output_full, preferred_element_type=jnp.float32)
    resid = tokens_float + residual_scale * attention_out
    scale_two = lax.rsqrt(jnp.mean(resid * resid, axis=-1, keepdims=True) + norm_eps)
    normed_two = (resid * scale_two * gain_two.astype(jnp.float32)).astype(jnp.bfloat16)

    normed_all = group_gather(normed_two, groups)
    logits = jnp.dot(normed_all, router_full, preferred_element_type=jnp.float32)
    chosen = jnp.any(
        routes_all[:, :, None] == jnp.arange(E, dtype=jnp.int32)[None, None, :], axis=1
    )
    shown = jnp.where(chosen, logits, -jnp.inf)
    gates = jax.nn.softmax(shown, axis=-1)
    first_expert = lax.axis_index("group") * local_experts
    gates_local = lax.dynamic_slice_in_dim(gates, first_expert, local_experts, 1)
    chunk = 2 * length
    parts = [
        run_experts(
            normed_all[start : start + chunk],
            cotangent_all[start : start + chunk],
            gates_local[start : start + chunk],
            gate_weight,
            up_weight,
            down_weight,
        )
        for start in range(0, normed_all.shape[0], chunk)
    ]
    moe_part, grad_rows_part, grad_gates = (
        jnp.concatenate([part[place] for part in parts], 0) for place in range(3)
    )
    grad_gates = grad_gates[:, :local_experts]
    gate_sum, up_sum, down_sum = (
        flat_rows(sum(part[place].astype(jnp.float32) for part in parts))
        if len(parts) > 1
        else flat_rows(parts[0][place])
        for place in range(3, 6)
    )
    down_sum = sum_step(down_sum, replicas, 0)
    moe_out = group_scatter(moe_part.astype(jnp.bfloat16), groups).astype(jnp.float32)
    layer_output = (resid + residual_scale * moe_out).astype(jnp.bfloat16)

    grad_chosen = gates_local * grad_gates
    grad_logits = lax.dynamic_update_slice_in_dim(
        jnp.zeros_like(gates), grad_chosen, first_expert, 1
    ) - gates * jnp.sum(grad_chosen, axis=-1, keepdims=True)
    grad_logits = grad_logits.astype(jnp.bfloat16)
    router_part = jnp.einsum(
        "sd,se->de", normed_all, grad_logits, preferred_element_type=jnp.float32
    )
    grad_normed_part = (
        grad_rows_part
        + jnp.einsum("se,de->sd", grad_logits, router_full, preferred_element_type=jnp.float32)
    )
    grad_normed_part, down_sum = lax.optimization_barrier(
        (grad_normed_part.astype(jnp.bfloat16), down_sum)
    )
    down_sum = sum_step(down_sum, replicas, 1)
    gate_sum = sum_step(gate_sum, replicas, 0)
    grad_normed_two = group_scatter(grad_normed_part, groups)
    grad_normed_two, gate_sum = lax.optimization_barrier((grad_normed_two, gate_sum))
    grad_normed_two = grad_normed_two.astype(jnp.float32)
    gate_sum = sum_step(gate_sum, replicas, 1)
    up_sum = sum_step(up_sum, replicas, 0, True)
    grad_out = cotangent.astype(jnp.float32)
    second_part = jnp.sum(grad_normed_two * resid * scale_two, axis=0)
    weighted_two = grad_normed_two * gain_two.astype(jnp.float32)
    grad_resid = (
        grad_out
        + scale_two * weighted_two
        - resid * scale_two**3 * jnp.mean(weighted_two * resid, axis=-1, keepdims=True)
    )
    grad_attention = (residual_scale * grad_resid).astype(jnp.bfloat16)
    output_part = jnp.einsum(
        "sk,sd->kd", attention_mix, grad_attention, preferred_element_type=jnp.float32
    )
    grad_mix = jnp.einsum(
        "sd,kd->sk", grad_attention, output_full, preferred_element_type=jnp.float32
    ).astype(jnp.bfloat16)
    grad_mix, up_sum, down_sum = lax.optimization_barrier((grad_mix, up_sum, down_sum))
    up_sum = sum_step(up_sum, replicas, 1, True)
    down_sum = sum_step(down_sum, replicas, 2)
    grad_wide = jnp.concatenate(
        attend_backward(projected, grad_mix, cosine_pair, sine_pair), 1
    )
    grad_wide, gate_sum, down_sum = lax.optimization_barrier((grad_wide, gate_sum, down_sum))
    gate_sum = sum_step(gate_sum, replicas, 2)
    down_sum = sum_step(down_sum, replicas, 3)
    grad_normed_one = jnp.einsum(
        "sk,dk->sd", grad_wide, wide_full, preferred_element_type=jnp.float32
    )
    first_part = jnp.sum(grad_normed_one * tokens_float * scale_one, axis=0)
    wide_part = jnp.einsum("sd,sk->dk", normed_one, grad_wide, preferred_element_type=jnp.float32)
    small_sum = jnp.concatenate(
        [
            wide_part.astype(jnp.bfloat16),
            output_part.astype(jnp.bfloat16),
            router_part.astype(jnp.bfloat16),
            second_part[:, None].astype(jnp.bfloat16),
            first_part[:, None].astype(jnp.bfloat16),
            jnp.zeros((wide_part.shape[0], spare), jnp.bfloat16),
        ],
        1,
    )
    rows = small_sum.shape[0] // groups
    small_sum = small_sum.reshape(groups, rows, small_sum.shape[1])
    states = [small_sum, up_sum, gate_sum, down_sum]
    places = [0, 2, 3, 4]
    while places[0] < 2 * len(bits_of(replicas)) + 1:
        for which in range(4):
            if which == 0:
                states[0] = small_step(states[0], replicas, groups, places[0])
            elif places[which] < 2 * len(bits_of(replicas)):
                states[which] = sum_step(states[which], replicas, places[which], which == 1)
            places[which] += 1
    small_sum = states[0][0].astype(jnp.float32)
    up_grad = states[1].reshape(up_weight.shape)
    gate_grad = states[2].reshape(gate_weight.shape)
    down_grad = states[3].reshape(down_weight.shape)
    weighted_one = grad_normed_one * gain_one.astype(jnp.float32)
    tokens_grad = (
        grad_resid
        + scale_one * weighted_one
        - tokens_float
        * scale_one**3
        * jnp.mean(weighted_one * tokens_float, axis=-1, keepdims=True)
    )
    wide_width = wide.shape[1]
    tail = wide_width + output_width
    return (
        layer_output,
        tokens_grad,
        small_sum[:, tail + E + 1],
        small_sum[:, :query_width],
        small_sum[:, query_width : query_width + key_width],
        small_sum[:, query_width + key_width : wide_width],
        small_sum[:, wide_width:tail],
        small_sum[:, tail + E],
        small_sum[:, tail : tail + E],
        gate_grad,
        up_grad,
        down_grad,
    )


def solution(mesh):
    return jax.shard_map(
        functools.partial(shards, mesh.shape["replica"], mesh.shape["group"]),
        mesh=mesh,
        in_specs=(
            P(("replica", "group"), None),
            P(("replica", "group"), None),
            P(("replica", "group"), None),
            P("group"),
            P("group", None),
            P("group", None),
            P("group", None),
            P("group", None),
            P("group"),
            P("group", None),
            P("group", None, None),
            P("group", None, None),
            P("group", None, None),
        ),
        out_specs=(
            P(("replica", "group"), None),
            P(("replica", "group"), None),
            P("group"),
            P("group", None),
            P("group", None),
            P("group", None),
            P("group", None),
            P("group"),
            P("group", None),
            P("group", None, None),
            P("group", None, None),
            P("group", None, None),
        ),
        check_vma=False,
    )
```

time: 1040 us -> 769 us (0.74)
  matrix products: 232 us -> 23 us
  Pallas kernels: 0 us -> 171 us
  waiting for transfers between devices: 430 us -> 350 us
  local copies, waits for them, and re-layouts: 148 us -> 82.3 us
  other arithmetic: 133 us -> 91.7 us
  loops' own time: 21.7 us -> 0 us
  starting transfers between devices: 53.8 us -> 39.4 us
    dot_general x65 -> x0, matrix products: 206 us -> none  [the longest x1 29 us: shards(): jnp.einsum('td,efd->etf', cotangent_all, down_weight, preferred_element_t...]
    pallas_call x0 -> x6, Pallas kernels: none -> 171 us  [the longest x1 104 us: run_experts(): pl.pallas_call(expert_kernel, grid=(experts,), in_specs=[whole_spec((leng...]
    ppermute x52 -> x43, waiting for transfers between devices: 430 us -> 350 us  [swap(): return lax.ppermute(values, axis, [(i, i ^ bit) for i in range(size)])]
    dynamic_slice x48 -> x1, local copies, waits for them, and re-layouts: 25 us -> 0.2 us  [shards(): lax.dynamic_slice_in_dim(gates, first_expert, local_experts, 1)]
    concatenate x23 -> x18, other arithmetic: 35.5 us -> 11.8 us  [unfold(): return jnp.concatenate([lower, upper], dim)]
    another operation x2 -> x0, loops' own time: 21.7 us -> none  [the longest x1 10.9 us: attend_backward(): lax.map(one_group, (jnp.arange(KV, dtype=jnp.int32), log_sums))]
    convert_element_type x2, local copies, waits for them, and re-layouts: 22.7 us -> 2.28 us  [the longest x1 1.14 us: shards(): second_part[:, None].astype(jnp.bfloat16)]
    convert_element_type x22 -> x18, other arithmetic: 22.8 us -> 38.3 us  [fold(): (keep.astype(jnp.float32) + received.astype(jnp.float32)).astype(jnp.bflo...]
  transfers between devices with their start and end apart: 52 -> 43, of which waited for: 26 -> 23; matrix products, arithmetic and copies ran while one was open for 34% -> 21% of each run, Pallas kernels for 0% -> 7%
where the time goes in v2:
time: 769 us; the launch traced here: 760 us
  waiting for transfers between devices  350 us (46%)
  Pallas kernels  171 us (22%)
  other arithmetic  91.7 us (12%)
  local copies, waits for them, and re-layouts  82.3 us (11%)
  starting transfers between devices  39.4 us (5%)
  matrix products  23 us (3%)
    ppermute x43, waiting for transfers between devices, swap(): return lax.ppermute(values, axis, [(i, i ^ bit) for i in range(size)])  350 us
    pallas_call x1, Pallas kernels, run_experts(): pl.pallas_call(expert_kernel, grid=(experts,), in_specs=[whole_spec((leng...  104 us
    ppermute x43, starting transfers between devices, swap(): return lax.ppermute(values, axis, [(i, i ^ bit) for i in range(size)])  39.4 us
    convert_element_type x18, other arithmetic, fold(): (keep.astype(jnp.float32) + received.astype(jnp.float32)).astype(jnp.bflo...  38.3 us
    pallas_call x3, Pallas kernels, join_halves(): pl.pallas_call(join_kernel, grid_spec=pltpu.PrefetchScalarGridSpec(num_sc...  33.8 us
    dynamic_slice x19, local copies, waits for them, and re-layouts, fold(): send = lax.dynamic_slice_in_dim(values, (1 - side) * half, half, dim)  28.5 us
    select_n x21, other arithmetic, unfold(): lower = jnp.where(side == 0, values, other)  19.1 us
    pallas_call x1, Pallas kernels, attend_backward(): pl.pallas_call(backward_kernel, grid=(KV // 2,), in_specs=[query_spec, ke...  18.8 us
  transfers between devices with their start and end apart: 43, of which 23 were waited for; matrix products, arithmetic and copies ran while one was open for 21% of the time, Pallas kernels for 7%

profile of v2, /device:TPU:0, one launch (start us, length us, event | category | flops | bytes accessed | tf_op | source)
XLA Modules:
  0.0 759.9 jit_solution(13436025912978869815)
XLA Ops:
  6.6 3.0 collective-permute-start.3
  14.1 10.0 %collective-permute-done.3 = bf16[1,256,1152]{2,1,0:T(8,128)(2,1)} collective-permute-done((bf16[1,256,1152]{2,1,0:T(8,128)(2,1)}, bf16[1,256,1152]{2,1,0:T(8,128)(2,1)}, u32[]{:S(2)}, u32[]{:S(2)}) %collective-permute-start.3) | collective-permute-done | bytes 589856 | tf_op jit(solution)/shard_map/ppermute | solution.py:37
  26.6 20.0 %collective-permute-done.1 = bf16[1,256,2048]{2,1,0:T(8,128)(2,1)} collective-permute-done((bf16[1,256,2048]{2,1,0:T(8,128)(2,1)}, bf16[1,256,2048]{2,1,0:T(8,128)(2,1)}, u32[]{:S(2)}, u32[]{:S(2)}) %collective-permute-start.1) | collective-permute-done | bytes 1048608 | tf_op jit(solution)/shard_map/ppermute | solution.py:37
  61.0 14.7 %shard_map.220 = bf16[512,1024]{1,0:T(8,128)(2,1)S(1)} custom-call(f32[512,2048]{1,0:T(8,128)S(1)} %fusion.32.query_ref.key_ref.value_ref, f32[512,2048]{1,0:T(8,128)S(1)} %fusion.32.query_ref.key_ref.value_ref, f32[512,2048]{1,0:T(8,128)S(1)} %fusion.32.query_ref.key_ref.value_ref, f32[512,128]{1,0:T(8,128)S(1)} %get-tuple-element.191.cos_ref, ...), custom_call_target="tpu_custom_call" | custom-call | flops 1073741824 | bytes 6291456 | tf_op jit(solution)/shard_map/pallas_call | solution.py:286
  80.9 24.1 %collective-permute-done.7 = s32[512,8]{0,1:T(8,128)S(1)} collective-permute-done((s32[512,8]{0,1:T(8,128)S(1)}, s32[512,8]{0,1:T(8,128)S(1)}, u32[]{:S(2)}, u32[]{:S(2)}) %collective-permute-start.7) | collective-permute-done | bytes 16416 | tf_op jit(solution)/shard_map/ppermute | solution.py:37
  116.3 4.0 copy.105.turned_ref
  121.3 103.6 %shard_map.221 = (f32[1024,1024]{1,0:T(8,128)}, f32[1024,1024]{1,0:T(8,128)}, f32[1024,128]{1,0:T(8,128)}, bf16[8,1024,512]{2,1,0:T(8,128)(2,1)}, bf16[8,1024,51...) custom-call(bf16[1024,1024]{1,0:T(8,128)(2,1)} %get-tuple-element.157.rows_ref, bf16[1024,1024]{1,0:T(8,128)(2,1)} %copy.105.turned_ref, ...), custom_call_target="tpu_custom_call" | custom-call | flops 77309411328 | bytes 50331648 | tf_op jit(solution)/shard_map/pallas_call | solution.py:407
  224.9 4.6 constant_dynamic-slice_fusion.17
  229.5 4.8 constant_dynamic-slice_fusion.14
  238.4 3.9 convert_element_type.277
  244.1 3.4 dynamic_update_slice.3
  260.1 4.3 add_convert_fusion.2
  268.6 7.1 add_convert_fusion
  275.7 3.5 add_convert_fusion.1
  279.2 22.8 %collective-permute-done.10 = bf16[512,1024]{1,0:T(8,128)(2,1)S(1)} collective-permute-done((bf16[512,1024]{1,0:T(8,128)(2,1)S(1)}, bf16[512,1024]{1,0:T(8,128)(2,1)S(1)}, u32[]{:S(2)}, u32[]{:S(2)}) %collective-permute-start.10) | collective-permute-done | bytes 1048608 | tf_op jit(solution)/shard_map/ppermute | solution.py:37
  306.1 3.3 fusion.4
  311.9 4.0 collective-permute-done.13
  315.9 3.3 add_convert_fusion.6
  326.6 18.8 %shard_map.222 = (bf16[512,1024]{1,0:T(8,128)(2,1)S(1)}, bf16[512,512]{1,0:T(8,128)(2,1)S(1)}, bf16[512,512]{1,0:T(8,128)(2,1)S(1)}) custom-call(f32[512,2048]{1,0:T(8,128)S(1)} %copy-done.1, f32[512,2048]{1,0:T(8,128)S(1)} %copy-done.1, f32[512,2048]{1,0:T(8,128)S(1)} %copy-done.1, bf16[512,1024]{1,0:T(8,128)(2,1)S(1)} %fusion.22.grad_ref, ...), custom_call_target="tpu_custom_call" | custom-call | flops 2684354560 | bytes 8388608 | tf_op jit(solution)/shard_map/pallas_call | solution.py:304
  347.1 12.5 %collective-permute-done.14 = bf16[2048,512]{1,0:T(8,128)(2,1)} collective-permute-done((bf16[2048,512]{1,0:T(8,128)(2,1)}, bf16[2048,512]{1,0:T(8,128)(2,1)}, u32[]{:S(2)}, u32[]{:S(2)}) %collective-permute-start.14) | collective-permute-done | bytes 2097184 | tf_op jit(solution)/shard_map/ppermute | solution.py:37
  361.9 3.9 fusion.15
  366.9 6.1 convolution_convert_fusion
  373.1 11.0 %concatenate.116 = bf16[2,512,3200]{2,1,0:T(8,128)(2,1)} concatenate(bf16[2,512,2048]{2,1,0:T(8,128)(2,1)} %bitcast.51, bf16[2,512,1024]{2,1,0:T(8,128)(2,1)} %bitcast.57, bf16[2,512,16]{2,1,0:T(8,128)(2,1)S(1)} %bitcast.58, bf16[2,512,1]{2,1,0:T(8,128)(2,1)} %convert_element_type.354, bf16[2,512,1]{2,1,0:T(8,128)(2,1)} %convert_element_type.355, ...), dimensions={2} | concatenate | bytes 13107200 | tf_op jit(solution)/shard_map/concatenate | solution.py:586
  384.1 4.0 constant_dynamic-slice_fusion.10
  394.1 21.7 %collective-permute-done.38 = bf16[256,1024]{1,0:T(8,128)(2,1)} collective-permute-done((bf16[256,1024]{1,0:T(8,128)(2,1)}, bf16[256,1024]{1,0:T(8,128)(2,1)}, u32[]{:S(2)}, u32[]{:S(2)}) %collective-permute-start.38) | collective-permute-done | bytes 524320 | tf_op jit(solution)/shard_map/ppermute | solution.py:37
  417.9 2.8 add_convert_fusion.4
  421.8 2.9 collective-permute-start.32
  424.7 10.3 %collective-permute-done.25 = bf16[1024,512]{1,0:T(8,128)(2,1)} collective-permute-done((bf16[1024,512]{1,0:T(8,128)(2,1)}, bf16[1024,512]{1,0:T(8,128)(2,1)}, u32[]{:S(2)}, u32[]{:S(2)}) %collective-permute-start.25) | collective-permute-done | bytes 1048608 | tf_op jit(solution)/shard_map/ppermute | solution.py:37
  437.8 41.0 %collective-permute-done.39 = bf16[256,1024]{1,0:T(8,128)(2,1)} collective-permute-done((bf16[256,1024]{1,0:T(8,128)(2,1)}, bf16[256,1024]{1,0:T(8,128)(2,1)}, u32[]{:S(2)}, u32[]{:S(2)}) %collective-permute-start.39) | collective-permute-done | bytes 524320 | tf_op jit(solution)/shard_map/ppermute | solution.py:37
  481.9 29.5 %collective-permute-done.26 = bf16[512,512]{1,0:T(8,128)(2,1)} collective-permute-done((bf16[512,512]{1,0:T(8,128)(2,1)}, bf16[512,512]{1,0:T(8,128)(2,1)}, u32[]{:S(2)}, u32[]{:S(2)}) %collective-permute-start.26) | collective-permute-done | bytes 524320 | tf_op jit(solution)/shard_map/ppermute | solution.py:37
  524.1 14.4 %collective-permute-done.27 = bf16[512,512]{1,0:T(8,128)(2,1)} collective-permute-done((bf16[512,512]{1,0:T(8,128)(2,1)}, bf16[512,512]{1,0:T(8,128)(2,1)}, u32[]{:S(2)}, u32[]{:S(2)}) %collective-permute-start.27) | collective-permute-done | bytes 524320 | tf_op jit(solution)/shard_map/ppermute | solution.py:37
  548.6 7.4 collective-permute-done.34
  556.2 3.3 collective-permute-done.17
  562.1 17.6 %collective-permute-done.28 = bf16[1024,512]{1,0:T(8,128)(2,1)S(1)} collective-permute-done((bf16[1024,512]{1,0:T(8,128)(2,1)S(1)}, bf16[1024,512]{1,0:T(8,128)(2,1)S(1)}, u32[]{:S(2)}, u32[]{:S(2)}) %collective-permute-start.28) | collective-permute-done | bytes 1048608 | tf_op jit(solution)/shard_map/ppermute | solution.py:37
  580.9 20.1 %collective-permute-done.41 = bf16[1024,1024]{1,0:T(8,128)(2,1)S(1)} collective-permute-done((bf16[1024,1024]{1,0:T(8,128)(2,1)S(1)}, bf16[1024,1024]{1,0:T(8,128)(2,1)S(1)}, u32[]{:S(2)}, u32[]{:S(2)}) %collective-permute-start.41) | collective-permute-done | bytes 2097184 | tf_op jit(solution)/shard_map/ppermute | solution.py:37
  602.1 16.3 %collective-permute-done.18 = bf16[1,128,3200]{2,1,0:T(8,128)(2,1)S(1)} collective-permute-done((bf16[1,128,3200]{2,1,0:T(8,128)(2,1)S(1)}, bf16[1,128,3200]{2,1,0:T(8,128)(2,1)S(1)}, u32[]{:S(2)}, u32[]{:S(2)}) %collective-permute-start.18) | collective-permute-done | bytes 819232 | tf_op jit(solution)/shard_map/ppermute | solution.py:37
  619.7 7.0 collective-permute-done.19
  630.3 6.0 collective-permute-done.20
  637.4 23.4 %collective-permute-done.29 = bf16[2048,512]{1,0:T(8,128)(2,1)S(1)} collective-permute-done((bf16[2048,512]{1,0:T(8,128)(2,1)S(1)}, bf16[2048,512]{1,0:T(8,128)(2,1)S(1)}, u32[]{:S(2)}, u32[]{:S(2)}) %collective-permute-start.29) | collective-permute-done | bytes 2097184 | tf_op jit(solution)/shard_map/ppermute | solution.py:37
  661.6 19.2 %collective-permute-done.21 = bf16[1,32,3200]{2,1,0:T(8,128)(2,1)S(1)} collective-permute-done((bf16[1,32,3200]{2,1,0:T(8,128)(2,1)S(1)}, bf16[1,32,3200]{2,1,0:T(8,128)(2,1)S(1)}, u32[]{:S(2)}, u32[]{:S(2)}) %collective-permute-start.21) | collective-permute-done | bytes 204832 | tf_op jit(solution)/shard_map/ppermute | solution.py:37
  684.4 5.4 collective-permute-done.22
  694.9 11.9 %collective-permute-done.23 = bf16[1,128,3200]{2,1,0:T(8,128)(2,1)S(1)} collective-permute-done((bf16[1,128,3200]{2,1,0:T(8,128)(2,1)S(1)}, bf16[1,128,3200]{2,1,0:T(8,128)(2,1)S(1)}, u32[]{:S(2)}, u32[]{:S(2)}) %collective-permute-start.23) | collective-permute-done | bytes 819232 | tf_op jit(solution)/shard_map/ppermute | solution.py:37
  711.2 6.5 shard_map.225
  718.7 2.8 copy-done.5
  724.2 3.0 fusion.44
  727.3 4.8 fusion.43
  732.1 13.7 %shard_map.223 = f32[8192,512]{1,0:T(8,128)} custom-call(s32[1]{0:T(128)} %bitcast.14.side_ref, bf16[4096,512]{1,0:T(8,128)(2,1)} %pad_maximum_fusion.1.own_ref, bf16[4096,512]{1,0:T(8,128)(2,1)} %collective-permute-done.30.other_ref), custom_call_target="tpu_custom_call" | custom-call | bytes 33554432 | tf_op jit(solution)/shard_map/pallas_call | solution.py:103
  745.8 13.7 %shard_map.224 = f32[8192,512]{1,0:T(8,128)} custom-call(s32[1]{0:T(128)} %bitcast.14.side_ref, bf16[4096,512]{1,0:T(8,128)(2,1)} %pad_maximum_fusion.2.own_ref, bf16[4096,512]{1,0:T(8,128)(2,1)} %collective-permute-done.37.other_ref), custom_call_target="tpu_custom_call" | custom-call | bytes 33554432 | tf_op jit(solution)/shard_map/pallas_call | solution.py:103
  (288 shorter events, 152.3 us)
Async XLA Ops:
  6.6 17.4 %collective-permute-start.3 = (bf16[1,256,1152]{2,1,0:T(8,128)(2,1)}, bf16[1,256,1152]{2,1,0:T(8,128)(2,1)}, u32[]{:S(2)}, u32[]{:S(2)}) collective-permute-start(bf16[1,256,1152]{2,1,0:T(8,128)(2,1)} %dynamic-slice_bitcast_fusion), channel_id=1, source_target_pairs={{0,1},{1,0},{2,3},{3,2},{4,5},{5,4},{6,7},{7,6},{8,9},{9,8},{10,11... | collective-permute-start | bytes 1769480 | tf_op jit(solution)/shard_map/ppermute | solution.py:37
  9.6 42.2 %collective-permute-start = (bf16[512]{0:T(512)(128)(2,1)S(1)}, bf16[512]{0:T(512)(128)(2,1)S(1)}, u32[]{:S(2)}, u32[]{:S(2)}) collective-permute-start(bf16[512]{0:T(512)(128)(2,1)S(1)} %copy-done.47), channel_id=1, source_target_pairs={{0,1},{1,0},{2,3},{3,2},{4,5},{5,4},{6,7},{7,6},{8,9},{9,8},{10,11... | collective-permute-start | bytes 3080 | tf_op jit(solution)/shard_map/ppermute | solution.py:37
  11.8 34.8 %collective-permute-start.1 = (bf16[1,256,2048]{2,1,0:T(8,128)(2,1)}, bf16[1,256,2048]{2,1,0:T(8,128)(2,1)}, u32[]{:S(2)}, u32[]{:S(2)}) collective-permute-start(bf16[1,256,2048]{2,1,0:T(8,128)(2,1)} %fusion.27), channel_id=1, source_target_pairs={{0,1},{1,0},{2,3},{3,2},{4,5},{5,4},{6,7},{7,6},{8,9},{9,8},{10,11... | collective-permute-start | bytes 3145736 | tf_op jit(solution)/shard_map/ppermute | solution.py:37
  13.7 91.6 %collective-permute-start.6 = (bf16[512,1024]{1,0:T(8,128)(2,1)}, bf16[512,1024]{1,0:T(8,128)(2,1)}, u32[]{:S(2)}, u32[]{:S(2)}) collective-permute-start(bf16[512,1024]{1,0:T(8,128)(2,1)} %param.14), channel_id=1, source_target_pairs={{0,1},{1,0},{2,3},{3,2},{4,5},{5,4},{6,7},{7,6},{8,9},{9,8},{10,11... | collective-permute-start | bytes 3145736 | tf_op jit(solution)/shard_map/ppermute | solution.py:37
  26.6 25.3 %collective-permute-start.4 = (bf16[2,256,1152]{2,1,0:T(8,128)(2,1)}, bf16[2,256,1152]{2,1,0:T(8,128)(2,1)}, u32[]{:S(2)}, u32[]{:S(2)}) collective-permute-start(bf16[2,256,1152]{2,1,0:T(8,128)(2,1)} %pad_maximum_fusion.13), channel_id=1, source_target_pairs={{0,2},{2,0},{4,6},{6,4},{8,10},{10,8},{12,14},{14,12},{16,18},{18,... | collective-permute-start | bytes 3538952 | tf_op jit(solution)/shard_map/ppermute | solution.py:37
  49.8 5.7 collective-permute-start.2
  78.7 29.8 %collective-permute-start.5 = (bf16[512,1024]{1,0:T(8,128)(2,1)S(1)}, bf16[512,1024]{1,0:T(8,128)(2,1)}, u32[]{:S(2)}, u32[]{:S(2)}) collective-permute-start(bf16[512,1024]{1,0:T(8,128)(2,1)S(1)} %multiply_convert_fusion.1), channel_id=1, source_target_pairs={{0,1},{1,0},{2,3},{3,2},{4,5},{5,4},{6,7},{7,6},{8,9},{9,8},{10,11... | collective-permute-start | bytes 3145736 | tf_op jit(solution)/shard_map/ppermute | solution.py:37
  80.8 24.2 %collective-permute-start.7 = (s32[512,8]{0,1:T(8,128)S(1)}, s32[512,8]{0,1:T(8,128)S(1)}, u32[]{:S(2)}, u32[]{:S(2)}) collective-permute-start(s32[512,8]{0,1:T(8,128)S(1)} %copy-done.45), channel_id=1, source_target_pairs={{0,1},{1,0},{2,3},{3,2},{4,5},{5,4},{6,7},{7,6},{8,9},{9,8},{10,11... | collective-permute-start | bytes 49160 | tf_op jit(solution)/shard_map/ppermute | solution.py:37
  229.5 29.5 %collective-permute-start.9 = (bf16[2048,1024]{1,0:T(8,128)(2,1)}, bf16[2048,1024]{1,0:T(8,128)(2,1)}, u32[]{:S(2)}, u32[]{:S(2)}) collective-permute-start(bf16[2048,1024]{1,0:T(8,128)(2,1)} %constant_dynamic-slice_fusion.17), channel_id=1, source_target_pairs={{0,2},{2,0},{4,6},{6,4},{8,10},{10,8},{12,14},{14,12},{16,18},{18,... | collective-permute-start | bytes 12582920 | tf_op jit(solution)/shard_map/ppermute | solution.py:37
  234.3 34.3 %collective-permute-start.12 = (bf16[4096,512]{1,0:T(8,128)(2,1)}, bf16[4096,512]{1,0:T(8,128)(2,1)}, u32[]{:S(2)}, u32[]{:S(2)}) collective-permute-start(bf16[4096,512]{1,0:T(8,128)(2,1)} %constant_dynamic-slice_fusion.14), channel_id=1, source_target_pairs={{0,2},{2,0},{4,6},{6,4},{8,10},{10,8},{12,14},{14,12},{16,18},{18,... | collective-permute-start | bytes 12582920 | tf_op jit(solution)/shard_map/ppermute | solution.py:37
  237.9 37.7 %collective-permute-start.11 = (bf16[4096,512]{1,0:T(8,128)(2,1)}, bf16[4096,512]{1,0:T(8,128)(2,1)}, u32[]{:S(2)}, u32[]{:S(2)}) collective-permute-start(bf16[4096,512]{1,0:T(8,128)(2,1)} %constant_dynamic-slice_fusion.15), channel_id=1, source_target_pairs={{0,2},{2,0},{4,6},{6,4},{8,10},{10,8},{12,14},{14,12},{16,18},{18,... | collective-permute-start | bytes 12582920 | tf_op jit(solution)/shard_map/ppermute | solution.py:37
  253.8 52.3 %collective-permute-start.8 = (bf16[512,1024]{1,0:T(8,128)(2,1)}, bf16[512,1024]{1,0:T(8,128)(2,1)S(1)}, u32[]{:S(2)}, u32[]{:S(2)}) collective-permute-start(bf16[512,1024]{1,0:T(8,128)(2,1)} %constant_dynamic-slice_fusion.18), channel_id=1, source_target_pairs={{0,1},{1,0},{2,3},{3,2},{4,5},{5,4},{6,7},{7,6},{8,9},{9,8},{10,11... | collective-permute-start | bytes 3145736 | tf_op jit(solution)/shard_map/ppermute | solution.py:37
  264.5 37.5 %collective-permute-start.10 = (bf16[512,1024]{1,0:T(8,128)(2,1)S(1)}, bf16[512,1024]{1,0:T(8,128)(2,1)S(1)}, u32[]{:S(2)}, u32[]{:S(2)}) collective-permute-start(bf16[512,1024]{1,0:T(8,128)(2,1)S(1)} %constant_dynamic-slice_fusion.16), channel_id=1, source_target_pairs={{0,1},{1,0},{2,3},{3,2},{4,5},{5,4},{6,7},{7,6},{8,9},{9,8},{10,11... | collective-permute-start | bytes 3145736 | tf_op jit(solution)/shard_map/ppermute | solution.py:37
  267.1 48.8 %collective-permute-start.13 = (bf16[1024,1024]{1,0:T(8,128)(2,1)}, bf16[1024,1024]{1,0:T(8,128)(2,1)}, u32[]{:S(2)}, u32[]{:S(2)}) collective-permute-start(bf16[1024,1024]{1,0:T(8,128)(2,1)} %constant_dynamic-slice_fusion.13), channel_id=1, source_target_pairs={{0,4},{2,6},{4,0},{6,2},{8,12},{10,14},{12,8},{14,10},{16,20},{18,... | collective-permute-start | bytes 6291464 | tf_op jit(solution)/shard_map/ppermute | solution.py:37
  303.9 55.8 %collective-permute-start.14 = (bf16[2048,512]{1,0:T(8,128)(2,1)}, bf16[2048,512]{1,0:T(8,128)(2,1)}, u32[]{:S(2)}, u32[]{:S(2)}) collective-permute-start(bf16[2048,512]{1,0:T(8,128)(2,1)} %constant_dynamic-slice_fusion.12), channel_id=1, source_target_pairs={{0,4},{2,6},{4,0},{6,2},{8,12},{10,14},{12,8},{14,10},{16,20},{18,... | collective-permute-start | bytes 6291464 | tf_op jit(solution)/shard_map/ppermute | solution.py:37
  319.4 26.3 %collective-permute-start.15 = (bf16[512,1024]{1,0:T(8,128)(2,1)S(1)}, bf16[512,1024]{1,0:T(8,128)(2,1)S(1)}, u32[]{:S(2)}, u32[]{:S(2)}) collective-permute-start(bf16[512,1024]{1,0:T(8,128)(2,1)S(1)} %constant_dynamic-slice_fusion.11), channel_id=1, source_target_pairs={{0,8},{2,10},{4,12},{6,14},{8,0},{10,2},{12,4},{14,6},{16,24},{18,... | collective-permute-start | bytes 3145736 | tf_op jit(solution)/shard_map/ppermute | solution.py:37
  325.2 92.7 %collective-permute-start.31 = (bf16[2048,512]{1,0:T(8,128)(2,1)}, bf16[2048,512]{1,0:T(8,128)(2,1)}, u32[]{:S(2)}, u32[]{:S(2)}) collective-permute-start(bf16[2048,512]{1,0:T(8,128)(2,1)} %constant_dynamic-slice_fusion.3), channel_id=1, source_target_pairs={{0,8},{2,10},{4,12},{6,14},{8,0},{10,2},{12,4},{14,6},{16,24},{18,... | collective-permute-start | bytes 6291464 | tf_op jit(solution)/shard_map/ppermute | solution.py:37
  361.8 29.7 %copy-start.12 = (bf16[2048,512]{1,0:T(8,128)(2,1)}, bf16[2048,512]{1,0:T(8,128)(2,1)S(1)}, u32[]{:S(2)}) copy-start(bf16[2048,512]{1,0:T(8,128)(2,1)S(1)} %add_convert_fusion.5) | copy-start | bytes 6291460
  388.1 129.2 %collective-permute-start.16 = (bf16[2,256,3200]{2,1,0:T(8,128)(2,1)}, bf16[2,256,3200]{2,1,0:T(8,128)(2,1)}, u32[]{:S(2)}, u32[]{:S(2)}) collective-permute-start(bf16[2,256,3200]{2,1,0:T(8,128)(2,1)} %constant_dynamic-slice_fusion.10), channel_id=1, source_target_pairs={{0,2},{2,0},{4,6},{6,4},{8,10},{10,8},{12,14},{14,12},{16,18},{18,... | collective-permute-start | bytes 9830408 | tf_op jit(solution)/shard_map/ppermute | solution.py:37
  388.9 26.9 %collective-permute-start.38 = (bf16[256,1024]{1,0:T(8,128)(2,1)}, bf16[256,1024]{1,0:T(8,128)(2,1)}, u32[]{:S(2)}, u32[]{:S(2)}) collective-permute-start(bf16[256,1024]{1,0:T(8,128)(2,1)} %constant_dynamic-slice_fusion), channel_id=1, source_target_pairs={{0,16},{2,18},{4,20},{6,22},{8,24},{10,26},{12,28},{14,30},{16,0},... | collective-permute-start | bytes 1572872 | tf_op jit(solution)/shard_map/ppermute | solution.py:37
  392.6 42.4 %collective-permute-start.25 = (bf16[1024,512]{1,0:T(8,128)(2,1)}, bf16[1024,512]{1,0:T(8,128)(2,1)}, u32[]{:S(2)}, u32[]{:S(2)}) collective-permute-start(bf16[1024,512]{1,0:T(8,128)(2,1)} %constant_dynamic-slice_fusion.5), channel_id=1, source_target_pairs={{0,8},{2,10},{4,12},{6,14},{8,0},{10,2},{12,4},{14,6},{16,24},{18,... | collective-permute-start | bytes 3145736 | tf_op jit(solution)/shard_map/ppermute | solution.py:37
  417.9 61.0 %collective-permute-start.39 = (bf16[256,1024]{1,0:T(8,128)(2,1)}, bf16[256,1024]{1,0:T(8,128)(2,1)}, u32[]{:S(2)}, u32[]{:S(2)}) collective-permute-start(bf16[256,1024]{1,0:T(8,128)(2,1)} %add_convert_fusion.16), channel_id=1, source_target_pairs={{0,16},{2,18},{4,20},{6,22},{8,24},{10,26},{12,28},{14,30},{16,0},... | collective-permute-start | bytes 1572872 | tf_op jit(solution)/shard_map/ppermute | solution.py:37
  421.8 91.6 %collective-permute-start.32 = (bf16[1024,512]{1,0:T(8,128)(2,1)}, bf16[1024,512]{1,0:T(8,128)(2,1)}, u32[]{:S(2)}, u32[]{:S(2)}) collective-permute-start(bf16[1024,512]{1,0:T(8,128)(2,1)} %constant_dynamic-slice_fusion.2), channel_id=1, source_target_pairs={{0,16},{2,18},{4,20},{6,22},{8,24},{10,26},{12,28},{14,30},{16,0},... | collective-permute-start | bytes 3145736 | tf_op jit(solution)/shard_map/ppermute | solution.py:37
  435.0 82.4 %slice-start = ((s8[6553600]{0:T(1024)(128)(4,1)}), s8[2359296]{0:T(1024)(128)(4,1)S(1)}, s32[]{:S(2)}) async-start(s8[6553600]{0:T(1024)(128)(4,1)} %bitcast.34), calls=%async_computation | async-start | bytes 4718592
  437.8 73.6 %collective-permute-start.26 = (bf16[512,512]{1,0:T(8,128)(2,1)}, bf16[512,512]{1,0:T(8,128)(2,1)}, u32[]{:S(2)}, u32[]{:S(2)}) collective-permute-start(bf16[512,512]{1,0:T(8,128)(2,1)} %constant_dynamic-slice_fusion.4), channel_id=1, source_target_pairs={{0,16},{2,18},{4,20},{6,22},{8,24},{10,26},{12,28},{14,30},{16,0},... | collective-permute-start | bytes 1572872 | tf_op jit(solution)/shard_map/ppermute | solution.py:37
  437.8 73.6 %copy-start.32 = (bf16[1024,512]{1,0:T(8,128)(2,1)S(1)}, bf16[1024,512]{1,0:T(8,128)(2,1)}, u32[]{:S(2)}) copy-start(bf16[1024,512]{1,0:T(8,128)(2,1)} %copy-done.31) | copy-start | bytes 3145732
  480.2 33.2 %copy-start.16 = (bf16[2048,512]{1,0:T(8,128)(2,1)S(1)}, bf16[2048,512]{1,0:T(8,128)(2,1)}, u32[]{:S(2)}) copy-start(bf16[2048,512]{1,0:T(8,128)(2,1)} %copy-done.15) | copy-start | bytes 6291460
  480.2 37.2 %slice-start.1 = ((s8[6553600]{0:T(1024)(128)(4,1)}), s8[4194304]{0:T(1024)(128)(4,1)S(1)}, s32[]{:S(2)}) async-start(s8[6553600]{0:T(1024)(128)(4,1)} %bitcast.34), calls=%async_computation.1 | async-start | bytes 8388608
  481.2 63.9 %collective-permute-start.40 = (bf16[512,1024]{1,0:T(8,128)(2,1)}, bf16[512,1024]{1,0:T(8,128)(2,1)}, u32[]{:S(2)}, u32[]{:S(2)}) collective-permute-start(bf16[512,1024]{1,0:T(8,128)(2,1)} %pad_maximum_fusion.16), channel_id=1, source_target_pairs={{0,8},{2,10},{4,12},{6,14},{8,0},{10,2},{12,4},{14,6},{16,24},{18,... | collective-permute-start | bytes 3145736 | tf_op jit(solution)/shard_map/ppermute | solution.py:37
  513.4 25.2 %collective-permute-start.27 = (bf16[512,512]{1,0:T(8,128)(2,1)}, bf16[512,512]{1,0:T(8,128)(2,1)}, u32[]{:S(2)}, u32[]{:S(2)}) collective-permute-start(bf16[512,512]{1,0:T(8,128)(2,1)} %add_convert_fusion.18), channel_id=1, source_target_pairs={{0,16},{2,18},{4,20},{6,22},{8,24},{10,26},{12,28},{14,30},{16,0},... | collective-permute-start | bytes 1572872 | tf_op jit(solution)/shard_map/ppermute | solution.py:37
  515.9 24.0 %collective-permute-start.33 = (bf16[512,512]{1,0:T(8,128)(2,1)}, bf16[512,512]{1,0:T(8,128)(2,1)}, u32[]{:S(2)}, u32[]{:S(2)}) collective-permute-start(bf16[512,512]{1,0:T(8,128)(2,1)} %constant_dynamic-slice_fusion.1), channel_id=1, source_target_pairs={{0,4},{2,6},{4,0},{6,2},{8,12},{10,14},{12,8},{14,10},{16,20},{18,... | collective-permute-start | bytes 1572872 | tf_op jit(solution)/shard_map/ppermute | solution.py:37
  523.1 36.5 %collective-permute-start.17 = (bf16[1,256,3200]{2,1,0:T(8,128)(2,1)}, bf16[1,256,3200]{2,1,0:T(8,128)(2,1)}, u32[]{:S(2)}, u32[]{:S(2)}) collective-permute-start(bf16[1,256,3200]{2,1,0:T(8,128)(2,1)} %constant_dynamic-slice_fusion.9), channel_id=1, source_target_pairs={{0,1},{1,0},{2,3},{3,2},{4,5},{5,4},{6,7},{7,6},{8,9},{9,8},{10,11... | collective-permute-start | bytes 4915208 | tf_op jit(solution)/shard_map/ppermute | solution.py:37
  541.1 14.9 %collective-permute-start.34 = (bf16[512,512]{1,0:T(8,128)(2,1)S(1)}, bf16[512,512]{1,0:T(8,128)(2,1)S(1)}, u32[]{:S(2)}, u32[]{:S(2)}) collective-permute-start(bf16[512,512]{1,0:T(8,128)(2,1)S(1)} %add_convert_fusion.17), channel_id=1, source_target_pairs={{0,4},{2,6},{4,0},{6,2},{8,12},{10,14},{12,8},{14,10},{16,20},{18,... | collective-permute-start | bytes 1572872 | tf_op jit(solution)/shard_map/ppermute | solution.py:37
  542.7 37.0 %collective-permute-start.28 = (bf16[1024,512]{1,0:T(8,128)(2,1)S(1)}, bf16[1024,512]{1,0:T(8,128)(2,1)S(1)}, u32[]{:S(2)}, u32[]{:S(2)}) collective-permute-start(bf16[1024,512]{1,0:T(8,128)(2,1)S(1)} %pad_maximum_fusion.14), channel_id=1, source_target_pairs={{0,8},{2,10},{4,12},{6,14},{8,0},{10,2},{12,4},{14,6},{16,24},{18,... | collective-permute-start | bytes 3145736 | tf_op jit(solution)/shard_map/ppermute | solution.py:37
  547.1 53.9 %collective-permute-start.41 = (bf16[1024,1024]{1,0:T(8,128)(2,1)S(1)}, bf16[1024,1024]{1,0:T(8,128)(2,1)S(1)}, u32[]{:S(2)}, u32[]{:S(2)}) collective-permute-start(bf16[1024,1024]{1,0:T(8,128)(2,1)S(1)} %pad_maximum_fusion.11), channel_id=1, source_target_pairs={{0,4},{2,6},{4,0},{6,2},{8,12},{10,14},{12,8},{14,10},{16,20},{18,... | collective-permute-start | bytes 6291464 | tf_op jit(solution)/shard_map/ppermute | solution.py:37
  556.1 63.2 %collective-permute-start.35 = (bf16[1024,512]{1,0:T(8,128)(2,1)S(1)}, bf16[1024,512]{1,0:T(8,128)(2,1)S(1)}, u32[]{:S(2)}, u32[]{:S(2)}) collective-permute-start(bf16[1024,512]{1,0:T(8,128)(2,1)S(1)} %pad_maximum_fusion.15), channel_id=1, source_target_pairs={{0,16},{2,18},{4,20},{6,22},{8,24},{10,26},{12,28},{14,30},{16,0},... | collective-permute-start | bytes 3145736 | tf_op jit(solution)/shard_map/ppermute | solution.py:37
  561.5 57.0 %collective-permute-start.18 = (bf16[1,128,3200]{2,1,0:T(8,128)(2,1)S(1)}, bf16[1,128,3200]{2,1,0:T(8,128)(2,1)S(1)}, u32[]{:S(2)}, u32[]{:S(2)}) collective-permute-start(bf16[1,128,3200]{2,1,0:T(8,128)(2,1)S(1)} %constant_dynamic-slice_fusion.8), channel_id=1, source_target_pairs={{0,4},{2,6},{4,0},{6,2},{8,12},{10,14},{12,8},{14,10},{16,20},{18,... | collective-permute-start | bytes 2457608 | tf_op jit(solution)/shard_map/ppermute | solution.py:37
  580.2 80.6 %collective-permute-start.29 = (bf16[2048,512]{1,0:T(8,128)(2,1)S(1)}, bf16[2048,512]{1,0:T(8,128)(2,1)S(1)}, u32[]{:S(2)}, u32[]{:S(2)}) collective-permute-start(bf16[2048,512]{1,0:T(8,128)(2,1)S(1)} %pad_maximum_fusion.9), channel_id=1, source_target_pairs={{0,4},{2,6},{4,0},{6,2},{8,12},{10,14},{12,8},{14,10},{16,20},{18,... | collective-permute-start | bytes 6291464 | tf_op jit(solution)/shard_map/ppermute | solution.py:37
  618.7 8.0 %collective-permute-start.19 = (bf16[1,64,3200]{2,1,0:T(8,128)(2,1)S(1)}, bf16[1,64,3200]{2,1,0:T(8,128)(2,1)S(1)}, u32[]{:S(2)}, u32[]{:S(2)}) collective-permute-start(bf16[1,64,3200]{2,1,0:T(8,128)(2,1)S(1)} %constant_dynamic-slice_fusion.7), channel_id=1, source_target_pairs={{0,8},{2,10},{4,12},{6,14},{8,0},{10,2},{12,4},{14,6},{16,24},{18,... | collective-permute-start | bytes 1228808 | tf_op jit(solution)/shard_map/ppermute | solution.py:37
  619.3 92.0 %collective-permute-start.42 = (bf16[2048,1024]{1,0:T(8,128)(2,1)S(1)}, bf16[2048,1024]{1,0:T(8,128)(2,1)S(1)}, u32[]{:S(2)}, u32[]{:S(2)}) collective-permute-start(bf16[2048,1024]{1,0:T(8,128)(2,1)S(1)} %pad_maximum_fusion.3.own_ref), channel_id=1, source_target_pairs={{0,2},{2,0},{4,6},{6,4},{8,10},{10,8},{12,14},{14,12},{16,18},{18,... | collective-permute-start | bytes 12582920 | tf_op jit(solution)/shard_map/ppermute | solution.py:37
  626.9 9.4 %collective-permute-start.20 = (bf16[1,32,3200]{2,1,0:T(8,128)(2,1)S(1)}, bf16[1,32,3200]{2,1,0:T(8,128)(2,1)S(1)}, u32[]{:S(2)}, u32[]{:S(2)}) collective-permute-start(bf16[1,32,3200]{2,1,0:T(8,128)(2,1)S(1)} %constant_dynamic-slice_fusion.6), channel_id=1, source_target_pairs={{0,16},{2,18},{4,20},{6,22},{8,24},{10,26},{12,28},{14,30},{16,0},... | collective-permute-start | bytes 614408 | tf_op jit(solution)/shard_map/ppermute | solution.py:37
  628.5 63.1 %collective-permute-start.36 = (bf16[2048,512]{1,0:T(8,128)(2,1)S(1)}, bf16[2048,512]{1,0:T(8,128)(2,1)S(1)}, u32[]{:S(2)}, u32[]{:S(2)}) collective-permute-start(bf16[2048,512]{1,0:T(8,128)(2,1)S(1)} %pad_maximum_fusion.10), channel_id=1, source_target_pairs={{0,8},{2,10},{4,12},{6,14},{8,0},{10,2},{12,4},{14,6},{16,24},{18,... | collective-permute-start | bytes 6291464 | tf_op jit(solution)/shard_map/ppermute | solution.py:37
  636.3 44.5 %collective-permute-start.21 = (bf16[1,32,3200]{2,1,0:T(8,128)(2,1)S(1)}, bf16[1,32,3200]{2,1,0:T(8,128)(2,1)S(1)}, u32[]{:S(2)}, u32[]{:S(2)}) collective-permute-start(bf16[1,32,3200]{2,1,0:T(8,128)(2,1)S(1)} %add_convert_fusion.20), channel_id=1, source_target_pairs={{0,16},{2,18},{4,20},{6,22},{8,24},{10,26},{12,28},{14,30},{16,0},... | collective-permute-start | bytes 614408 | tf_op jit(solution)/shard_map/ppermute | solution.py:37
  680.9 8.9 %collective-permute-start.22 = (bf16[1,64,3200]{2,1,0:T(8,128)(2,1)S(1)}, bf16[1,64,3200]{2,1,0:T(8,128)(2,1)S(1)}, u32[]{:S(2)}, u32[]{:S(2)}) collective-permute-start(bf16[1,64,3200]{2,1,0:T(8,128)(2,1)S(1)} %pad_maximum_fusion.18), channel_id=1, source_target_pairs={{0,8},{2,10},{4,12},{6,14},{8,0},{10,2},{12,4},{14,6},{16,24},{18,... | collective-permute-start | bytes 1228808 | tf_op jit(solution)/shard_map/ppermute | solution.py:37
  684.4 47.7 %collective-permute-start.30 = (bf16[4096,512]{1,0:T(8,128)(2,1)}, bf16[4096,512]{1,0:T(8,128)(2,1)}, u32[]{:S(2)}, u32[]{:S(2)}) collective-permute-start(bf16[4096,512]{1,0:T(8,128)(2,1)} %pad_maximum_fusion.1.own_ref), channel_id=1, source_target_pairs={{0,2},{2,0},{4,6},{6,4},{8,10},{10,8},{12,14},{14,12},{16,18},{18,... | collective-permute-start | bytes 12582920 | tf_op jit(solution)/shard_map/ppermute | solution.py:37
  690.0 16.7 %collective-permute-start.23 = (bf16[1,128,3200]{2,1,0:T(8,128)(2,1)S(1)}, bf16[1,128,3200]{2,1,0:T(8,128)(2,1)S(1)}, u32[]{:S(2)}, u32[]{:S(2)}) collective-permute-start(bf16[1,128,3200]{2,1,0:T(8,128)(2,1)S(1)} %pad_maximum_fusion.17), channel_id=1, source_target_pairs={{0,4},{2,6},{4,0},{6,2},{8,12},{10,14},{12,8},{14,10},{16,20},{18,... | collective-permute-start | bytes 2457608 | tf_op jit(solution)/shard_map/ppermute | solution.py:37
  694.9 50.9 %collective-permute-start.37 = (bf16[4096,512]{1,0:T(8,128)(2,1)}, bf16[4096,512]{1,0:T(8,128)(2,1)}, u32[]{:S(2)}, u32[]{:S(2)}) collective-permute-start(bf16[4096,512]{1,0:T(8,128)(2,1)} %pad_maximum_fusion.2.own_ref), channel_id=1, source_target_pairs={{0,2},{2,0},{4,6},{6,4},{8,10},{10,8},{12,14},{14,12},{16,18},{18,... | collective-permute-start | bytes 12582920 | tf_op jit(solution)/shard_map/ppermute | solution.py:37
  707.2 10.5 %collective-permute-start.24 = (bf16[1,256,3200]{2,1,0:T(8,128)(2,1)S(1)}, bf16[1,256,3200]{2,1,0:T(8,128)(2,1)S(1)}, u32[]{:S(2)}, u32[]{:S(2)}) collective-permute-start(bf16[1,256,3200]{2,1,0:T(8,128)(2,1)S(1)} %pad_maximum_fusion.12), channel_id=1, source_target_pairs={{0,2},{2,0},{4,6},{6,4},{8,10},{10,8},{12,14},{14,12},{16,18},{18,... | collective-permute-start | bytes 4915208 | tf_op jit(solution)/shard_map/ppermute | solution.py:37
  (49 other events, 308.8 us)
